TPU v7x, 128 devices: a whole 4x4x4 slice. The times are simulated.
128 devices in a mesh: gx: 8 (over x_lo, z), gy: 8 (over x_hi, y), gz: 2 (over core).
Axes of the slice: x: 4 (x_hi: 2, x_lo: 2; x = x_hi * 2 + x_lo), y: 4, z: 4, core: 2. Of those that a mesh axis runs over, the one named last changes fastest.
Arguments:
- iterate: float32 [128, 512, 256], P('gx', 'gy', 'gz'), may hold values from -8 to 8
- right_side: float32 [128, 512, 256], P('gx', 'gy', 'gz'), may hold values from -4 to 4
- diffusion: float32 [128, 512, 256], P('gx', 'gy', 'gz'), may hold values from 0.5 to 4
Outputs:
- improved: float32 [128, 512, 256], P('gx', 'gy', 'gz')
All inputs are finite; a program needn't handle non-finite values.
Results may differ from a plain program's by a relative error of at most 0.00002.
Values sent between devices are 32-bit elements; how exact they have to be, the bound alone decides.
A program may use at most 128 MiB of HBM per device.

v0:
```python
import jax
import jax.numpy as jnp
from jax import lax
from jax.sharding import PartitionSpec as P

DEGREE = 4
BOTTOM = 8


SMOOTH_LOW = 0.25
SMOOTH_HIGH = 2.0
BOTTOM_LOW = 0.05


def padded_2(cells, sides, width):
    for axis, dim in sides:
        count = lax.axis_size(axis)
        ends = count - 1
        head = lax.slice_in_dim(cells, 0, width, axis=dim)
        tail = lax.slice_in_dim(cells, cells.shape[dim] - width, cells.shape[dim], axis=dim)
        cells = jnp.concatenate(
            [
                lax.ppermute(tail, axis, [(i, (i + 1) % count) for i in range(ends)]),
                cells,
                lax.ppermute(head, axis, [((i + 1) % count, i) for i in range(ends)]),
            ],
            axis=dim,
        )
    return cells


def chebyshev_steps(sweeps, low_end, high_end):
    center = 0.5 * (high_end + low_end)
    radius = 0.5 * (high_end - low_end)
    sigma_ratio = center / radius
    rho_old = 1.0 / sigma_ratio
    steps_out = [(0.0, 1.0 / center)]
    for sweep_index in range(1, sweeps):
        rho_new = 1.0 / (2.0 * sigma_ratio - rho_old)
        steps_out.append((rho_new * rho_old, 2.0 * rho_new / radius))
        rho_old = rho_new
    return steps_out


def neighbour_views(padded):
    return (
        padded[:-2, 1:-1, 1:-1],
        padded[2:, 1:-1, 1:-1],
        padded[1:-1, :-2, 1:-1],
        padded[1:-1, 2:, 1:-1],
        padded[1:-1, 1:-1, :-2],
        padded[1:-1, 1:-1, 2:],
    )


def operate(padded_values, padded_beta, level_scale):
    centre_values = padded_values[1:-1, 1:-1, 1:-1]
    centre_beta = padded_beta[1:-1, 1:-1, 1:-1]
    accumulated = jnp.zeros_like(centre_values)
    for value_side, beta_side in zip(neighbour_views(padded_values), neighbour_views(padded_beta)):
        accumulated = accumulated + 0.5 * (centre_beta + beta_side) * (centre_values - value_side)
    return level_scale * accumulated


def diagonal_inverse(padded_beta, level_scale):
    centre_beta = padded_beta[1:-1, 1:-1, 1:-1]
    accumulated = jnp.zeros_like(centre_beta)
    for beta_side in neighbour_views(padded_beta):
        accumulated = accumulated + 0.5 * (centre_beta + beta_side)
    return 1.0 / (level_scale * accumulated)


def smooth(
    values, source, padded_beta, inverse, level_scale, sweeps, low_end, pad_values, start_zero
):
    weights = chebyshev_steps(sweeps, low_end, SMOOTH_HIGH)
    direction = jnp.zeros_like(values)
    if start_zero:
        direction = weights[0][1] * (inverse * source)
        values = direction
        weights = weights[1:]
    keep_weights = jnp.array([item[0] for item in weights], jnp.float32)
    new_weights = jnp.array([item[1] for item in weights], jnp.float32)

    def sweep_once(carry, pair):
        current, previous = carry
        residual = source - operate(pad_values(current), padded_beta, level_scale)
        update = pair[0] * previous + pair[1] * (inverse * residual)
        return ((current + update, update), None)

    (values, direction), unused = lax.scan(
        sweep_once, (values, direction), (keep_weights, new_weights)
    )
    return values


def restrict_cells(values):
    size_x, size_y, size_z = values.shape
    blocks = values.reshape(size_x // 2, 2, size_y // 2, 2, size_z // 2, 2)
    return jnp.mean(blocks, axis=(1, 3, 5))


def prolong_cells(values):
    return jnp.repeat(jnp.repeat(jnp.repeat(values, 2, axis=0), 2, axis=1), 2, axis=2)


def pad_whole(values):
    return jnp.pad(values, 1)


def pad_brick(values):
    return padded_2(values, (("gx", 0), ("gy", 1), ("gz", 2)), 1)


def pad_slab(values):
    inner_padded = padded_2(values, (("gy", 1),), 1)
    return jnp.pad(inner_padded, ((1, 1), (0, 0), (1, 1)))


def level_setup(beta_level, level_scale, pad_values):
    padded = pad_values(beta_level)
    return (padded, diagonal_inverse(padded, level_scale))


def bottom_solve(source, beta_level):
    padded, inverse = level_setup(beta_level, 0.015625, pad_whole)
    return smooth(
        jnp.zeros_like(source),
        source,
        padded,
        inverse,
        0.015625,
        BOTTOM,
        BOTTOM_LOW,
        pad_whole,
        True,
    )


def assemble_slab(gathered, count_x, count_z):
    width_x, width_y, width_z = gathered.shape[1:]
    arranged = gathered.reshape(count_x, count_z, width_x, width_y, width_z)
    return arranged.transpose(0, 2, 3, 1, 4).reshape(count_x * width_x, width_y, count_z * width_z)


def on_device(iterate, right_side, diffusion):
    count_x = lax.axis_size("gx")
    count_z = lax.axis_size("gz")
    beta_one = restrict_cells(diffusion)
    beta_two = restrict_cells(beta_one)
    padded_zero, inverse_zero = level_setup(diffusion, 1.0, pad_brick)
    padded_one, inverse_one = level_setup(beta_one, 0.25, pad_brick)
    presmoothed = smooth(
        iterate, right_side, padded_zero, inverse_zero, 1.0, DEGREE, SMOOTH_LOW, pad_brick, False
    )
    source_one = restrict_cells(right_side - operate(pad_brick(presmoothed), padded_zero, 1.0))
    correction_one = smooth(
        jnp.zeros_like(source_one),
        source_one,
        padded_one,
        inverse_one,
        0.25,
        DEGREE,
        SMOOTH_LOW,
        pad_brick,
        True,
    )
    brick_source = restrict_cells(source_one - operate(pad_brick(correction_one), padded_one, 0.25))
    gathered_source, gathered_beta = (
        lax.all_gather(brick_source[None], ("gx", "gz"), axis=0, tiled=True),
        lax.all_gather(beta_two[None], ("gx", "gz"), axis=0, tiled=True),
    )
    source_two = assemble_slab(gathered_source, count_x, count_z)
    slab_beta = assemble_slab(gathered_beta, count_x, count_z)
    padded_two, inverse_two = level_setup(slab_beta, 0.0625, pad_slab)
    correction_two = smooth(
        jnp.zeros_like(source_two),
        source_two,
        padded_two,
        inverse_two,
        0.0625,
        DEGREE,
        SMOOTH_LOW,
        pad_slab,
        True,
    )
    part_source = restrict_cells(source_two - operate(pad_slab(correction_two), padded_two, 0.0625))
    source_three, beta_three = (
        lax.all_gather(part_source, "gy", axis=1, tiled=True),
        lax.all_gather(restrict_cells(slab_beta), "gy", axis=1, tiled=True),
    )
    coarsest = bottom_solve(source_three, beta_three)
    slab_rows = part_source.shape[1]
    own_part = lax.dynamic_slice_in_dim(coarsest, lax.axis_index("gy") * slab_rows, slab_rows, 1)
    corrected_slab = smooth(
        correction_two + prolong_cells(own_part),
        source_two,
        padded_two,
        inverse_two,
        0.0625,
        DEGREE,
        SMOOTH_LOW,
        pad_slab,
        False,
    )
    brick_shape = beta_two.shape
    corrected_two = lax.dynamic_slice(
        corrected_slab,
        (lax.axis_index("gx") * brick_shape[0], 0, lax.axis_index("gz") * brick_shape[2]),
        brick_shape,
    )
    corrected_one = smooth(
        correction_one + prolong_cells(corrected_two),
        source_one,
        padded_one,
        inverse_one,
        0.25,
        DEGREE,
        SMOOTH_LOW,
        pad_brick,
        False,
    )
    return smooth(
        presmoothed + prolong_cells(corrected_one),
        right_side,
        padded_zero,
        inverse_zero,
        1.0,
        DEGREE,
        SMOOTH_LOW,
        pad_brick,
        False,
    )


def solution(mesh):
    placed = (P("gx", "gy", "gz"), P("gx", "gy", "gz"), P("gx", "gy", "gz"))
    return jax.shard_map(
        on_device, mesh=mesh, in_specs=placed, out_specs=P("gx", "gy", "gz"), check_vma=False
    )
```

profile of v0, /device:TPU:5, one launch (start us, length us, event | category | flops | bytes accessed | tf_op | source)
XLA Modules:
  0.0 1177.8 jit_solution(15938051661125128645)
XLA Ops:
  7.5 35.6 %reshape.73 = f32[8,2,32,2,64,2]{5,4,3,2,1,0:T(8,128)} reshape(f32[16,64,128]{2,1,0:T(8,128)} %param.33) | data formatting | bytes 1048576 | tf_op jit(solution)/shard_map/reshape | solution.py:99
  43.1 12.2 %reduce_sum.54 = f32[8,32,64]{2,1,0:T(8,128)S(1)} reduce(f32[8,2,32,2,64,2]{5,4,3,2,1,0:T(8,128)} %reshape.73, f32[]{:T(128)} %constant.191.clone.1), dimensions={1,3,5}, to_apply=%region_2.3 | reduce | flops 114688 | bytes 589828 | tf_op jit(solution)/shard_map/reduce_sum | solution.py:100
  61.0 5.7 div.55
  69.2 23.9 %all-gather = f32[64,16,32]{2,1,0:T(8,128)S(1)} all-gather(f32[4,16,32]{2,1,0:T(8,128)S(1)} %broadcast_multiply_fusion.5), channel_id=2, replica_groups=mesh['gx'=8,'gy'=8,'gz'=2] {'gx','gz'}, dimensions={0}, use_global_device_ids=true | all-gather | bytes 139264 | tf_op jit(solution)/shard_map/all_gather | solution.py:171
  97.2 5.7 collective-permute-start.31
  103.6 6.3 reshape_reshape.3
  116.6 7.0 collective-permute-start.47
  137.0 161.5 %while.112 = (s32[]{:T(128)}, f32[16,64,128]{2,1,0:T(8,128)}, f32[16,64,128]{2,1,0:T(8,128)}, f32[16,64,128]{2,1,0:T(8,128)}, f32[16,64,128]{2,1,0:T(8,128)S(1)}...) while((s32[]{:T(128)}, f32[16,64,128]{2,1,0:T(8,128)}, ...), condition=%wide.region_1.0_spmd.clone.clone, body=%wide.region_0.0_spmd.sunk.clone.clone.sunk | while | flops 5547011 | bytes 13378083 | solution.py:91
  144.4 7.2 collective-permute-start.10
  153.5 6.1 collective-permute-done.11
  172.5 5.6 fusion.317
  199.6 5.6 collective-permute-start.12
  211.5 5.7 fusion.317
  252.7 5.7 fusion.317
  292.8 5.7 fusion.317
  313.6 5.5 collective-permute-start.43
  320.6 6.1 collective-permute-start.39
  347.5 35.6 %reshape.74 = f32[8,2,32,2,64,2]{5,4,3,2,1,0:T(8,128)} reshape(f32[16,64,128]{2,1,0:T(8,128)} %fusion.159) | data formatting | bytes 1048576 | tf_op jit(solution)/shard_map/reshape | solution.py:99
  383.1 12.3 %reduce_sum.55 = f32[8,32,64]{2,1,0:T(8,128)S(1)} reduce(f32[8,2,32,2,64,2]{5,4,3,2,1,0:T(8,128)} %reshape.74, f32[]{:T(128)} %constant.191.clone.1), dimensions={1,3,5}, to_apply=%region_3.4 | reduce | flops 114688 | bytes 589828 | tf_op jit(solution)/shard_map/reduce_sum | solution.py:100
  396.9 105.1 %while.109 = (s32[]{:T(128)}, f32[8,32,64]{2,1,0:T(8,128)}, f32[8,32,64]{2,1,0:T(8,128)}, f32[8,32,64]{2,1,0:T(8,128)S(1)}, f32[8,32,64]{2,1,0:T(8,128)S(1)}, /*...) while((s32[]{:T(128)}, f32[8,32,64]{2,1,0:T(8,128)}, ...), condition=%wide.region_5.6_spmd.clone, body=%wide.region_4.5_spmd.sunk.clone.sunk | while | flops 698882 | bytes 2044005 | solution.py:91
  411.9 5.7 collective-permute-done.3
  452.7 6.7 collective-permute-start.4
  487.7 6.7 collective-permute-start.4
  515.0 7.0 collective-permute-start.51
  524.7 5.5 collective-permute-start.53
  534.4 5.7 reshape.77
  542.7 18.9 %all-gather.1 = f32[64,16,32]{2,1,0:T(8,128)S(1)} all-gather(f32[4,16,32]{2,1,0:T(8,128)S(1)} %broadcast_multiply_fusion.4), channel_id=3, replica_groups=mesh['gx'=8,'gy'=8,'gz'=2] {'gx','gz'}, dimensions={0}, use_global_device_ids=true | all-gather | bytes 139264 | tf_op jit(solution)/shard_map/all_gather | solution.py:170
  567.1 58.6 %while.110 = (s32[]{:T(128)}, f32[32,16,64]{2,1,0:T(8,128)}, f32[32,16,64]{2,1,0:T(8,128)}, f32[32,16,64]{2,1,0:T(8,128)S(1)}, f32[32,16,64]{2,1,0:T(8,128)S(1)}...) while((s32[]{:T(128)}, f32[32,16,64]{2,1,0:T(8,128)}, ...), condition=%wide.region_9.10_spmd.clone, body=%wide.region_8.9_spmd.sunk.clone.sunk | while | flops 1654458 | bytes 2783253 | solution.py:91
  568.7 7.5 collective-permute-start.6
  628.6 7.0 collective-permute-start.55
  635.6 31.5 %all_gather.14 = f32[16,64,32]{2,1,0:T(8,128)} all-gather(f32[16,8,32]{2,1,0:T(8,128)} %broadcast_multiply_fusion.3), channel_id=1, replica_groups=mesh['gx'=8,'gy'=8,'gz'=2] {'gy'}, dimensions={1}, use_global_device_ids=true | all-gather | bytes 147456 | tf_op jit(solution)/shard_map/all_gather | solution.py:190
  677.0 10.1 reshape.80
  691.1 28.5 %all_gather.15 = f32[16,64,32]{2,1,0:T(8,128)S(1)} all-gather(f32[16,8,32]{2,1,0:T(8,128)S(1)} %broadcast_multiply_fusion.2), channel_id=1, replica_groups=mesh['gx'=8,'gy'=8,'gz'=2] {'gy'}, dimensions={1}, use_global_device_ids=true | all-gather | bytes 147456 | tf_op jit(solution)/shard_map/all_gather | solution.py:189
  725.7 53.0 %while.111 = (s32[]{:T(128)}, f32[16,64,32]{2,1,0:T(8,128)}, f32[16,64,32]{2,1,0:T(8,128)}, f32[16,64,32]{2,1,0:T(8,128)}, f32[16,64,32]{2,1,0:T(8,128)}, /*inde...) while((s32[]{:T(128)}, f32[16,64,32]{2,1,0:T(8,128)}, ...), condition=%wide.region_13.14_spmd.clone, body=%wide.region_12.13_spmd.sunk.clone.sunk | while | flops 983042 | bytes 1835173 | solution.py:91
  783.7 70.9 %while.113 = (s32[]{:T(128)}, f32[32,16,64]{2,1,0:T(8,128)}, f32[32,16,64]{2,1,0:T(8,128)}, f32[32,16,64]{2,1,0:T(8,128)S(1)}, f32[32,16,64]{2,1,0:T(8,128)S(1)}...) while((s32[]{:T(128)}, f32[32,16,64]{2,1,0:T(8,128)}, ...), condition=%wide.region_15.16_spmd.clone.clone, body=%wide.region_14.15_spmd.sunk.clone.clone.sunk | while | flops 1687227 | bytes 2783271 | solution.py:91
  856.7 150.0 %while.114 = (s32[]{:T(128)}, f32[8,32,64]{2,1,0:T(8,128)S(1)}, f32[8,32,64]{2,1,0:T(8,128)}, f32[8,32,64]{2,1,0:T(8,128)S(1)}, f32[8,32,64]{2,1,0:T(8,128)}, /*...) while((s32[]{:T(128)}, f32[8,32,64]{2,1,0:T(8,128)S(1)}, ...), condition=%wide.region_17.18_spmd.clone.clone, body=%wide.region_16.17_spmd.sunk.clone.clone.sunk | while | flops 715267 | bytes 1662983 | solution.py:91
  868.5 6.0 collective-permute-done.19
  874.7 22.3 %collective-permute-start.20 = (f32[10,34,1]{2,1,0:T(8,128)S(1)}, f32[10,34,1]{2,1,0:T(8,128)}, u32[]{:S(2)}, u32[]{:S(2)}) collective-permute-start(f32[10,34,1]{2,1,0:T(8,128)S(1)} %get-tuple-element.2306), channel_id=1, source_target_pairs={{1,0},{3,2},{5,4},{7,6},{9,8},{11,10},{13,12},{15,14},{17,16},{19,... | collective-permute-start | bytes 4088 | tf_op jit(solution)/shard_map/while/body/eval_jaxpr/ppermute | solution.py:25
  909.3 5.7 collective-permute-done.17
  925.1 6.7 collective-permute-start.20
  939.2 5.7 collective-permute-start.16
  959.8 6.7 collective-permute-start.20
  992.7 6.7 collective-permute-start.20
  1013.9 164.0 %while.115 = (s32[]{:T(128)}, f32[16,64,128]{2,1,0:T(8,128)}, f32[16,64,128]{2,1,0:T(8,128)}, f32[16,64,128]{2,1,0:T(8,128)}, f32[16,64,128]{2,1,0:T(8,128)S(1)}...) while((s32[]{:T(128)}, f32[16,64,128]{2,1,0:T(8,128)}, ...), condition=%wide.region_19.20_spmd.clone.clone, body=%wide.region_18.19_spmd.sunk.clone.clone.sunk | while | flops 5547011 | bytes 13378083 | solution.py:91
  1036.2 6.0 collective-permute-start.26
  1090.5 5.6 fusion.327
  1131.3 5.6 fusion.327
  1172.2 5.6 fusion.327
  (689 shorter events, 754.5 us)
Async XLA Ops:
  2.7 91.2 %collective-permute-start.28 = (f32[1,64,128]{2,1,0:T(8,128)S(1)}, f32[1,64,128]{2,1,0:T(8,128)S(1)}, u32[]{:S(2)}, u32[]{:S(2)}) collective-permute-start(f32[1,64,128]{2,1,0:T(8,128)S(1)} %get-tuple-element.1757), channel_id=1, source_target_pairs={{0,16},{16,32},{32,48},{48,64},{64,80},{80,96},{96,112},{1,17},{17... | collective-permute-start | bytes 98312 | tf_op jit(solution)/shard_map/ppermute | solution.py:23
  6.2 87.8 %collective-permute-start.29 = (f32[1,64,128]{2,1,0:T(8,128)S(1)}, f32[1,64,128]{2,1,0:T(8,128)S(1)}, u32[]{:S(2)}, u32[]{:S(2)}) collective-permute-start(f32[1,64,128]{2,1,0:T(8,128)S(1)} %get-tuple-element.1756), channel_id=1, source_target_pairs={{16,0},{32,16},{48,32},{64,48},{80,64},{96,80},{112,96},{17,1},{33... | collective-permute-start | bytes 98312 | tf_op jit(solution)/shard_map/ppermute | solution.py:25
  55.4 70.4 %collective-permute-start.34 = (f32[1,32,64]{2,1,0:T(8,128)S(1)}, f32[1,32,64]{2,1,0:T(8,128)S(1)}, u32[]{:S(2)}, u32[]{:S(2)}) collective-permute-start(f32[1,32,64]{2,1,0:T(8,128)S(1)} %get-tuple-element.1775), channel_id=1, source_target_pairs={{0,16},{16,32},{32,48},{48,64},{64,80},{80,96},{96,112},{1,17},{17... | collective-permute-start | bytes 24584 | tf_op jit(solution)/shard_map/ppermute | solution.py:23
  59.7 69.3 %collective-permute-start.35 = (f32[1,32,64]{2,1,0:T(8,128)S(1)}, f32[1,32,64]{2,1,0:T(8,128)S(1)}, u32[]{:S(2)}, u32[]{:S(2)}) collective-permute-start(f32[1,32,64]{2,1,0:T(8,128)S(1)} %get-tuple-element.1774), channel_id=1, source_target_pairs={{16,0},{32,16},{48,32},{64,48},{80,64},{96,80},{112,96},{17,1},{33... | collective-permute-start | bytes 24584 | tf_op jit(solution)/shard_map/ppermute | solution.py:25
  94.0 22.5 %collective-permute-start.30 = (f32[18,1,128]{2,1,0:T(1,128)S(1)}, f32[18,1,128]{2,1,0:T(1,128)S(1)}, u32[]{:S(2)}, u32[]{:S(2)}) collective-permute-start(f32[18,1,128]{2,1,0:T(1,128)S(1)} %get-tuple-element.1752), channel_id=1, source_target_pairs={{0,2},{2,4},{4,6},{6,8},{8,10},{10,12},{12,14},{1,3},{3,5},{5,7},{... | collective-permute-start | bytes 27656 | tf_op jit(solution)/shard_map/ppermute | solution.py:23
  97.2 26.3 %collective-permute-start.31 = (f32[18,1,128]{2,1,0:T(1,128)S(1)}, f32[18,1,128]{2,1,0:T(1,128)S(1)}, u32[]{:S(2)}, u32[]{:S(2)}) collective-permute-start(f32[18,1,128]{2,1,0:T(1,128)S(1)} %get-tuple-element.1753), channel_id=1, source_target_pairs={{2,0},{4,2},{6,4},{8,6},{10,8},{12,10},{14,12},{3,1},{5,3},{7,5},{... | collective-permute-start | bytes 27656 | tf_op jit(solution)/shard_map/ppermute | solution.py:25
  114.5 407.5 %collective-permute-start.46 = (f32[32,1,64]{2,1,0:T(1,128)}, f32[32,1,64]{2,1,0:T(1,128)}, u32[]{:S(2)}, u32[]{:S(2)}) collective-permute-start(f32[32,1,64]{2,1,0:T(1,128)} %get-tuple-element.1760), channel_id=1, source_target_pairs={{0,2},{2,4},{4,6},{6,8},{8,10},{10,12},{12,14},{1,3},{3,5},{5,7},{... | collective-permute-start | bytes 24584 | tf_op jit(solution)/shard_map/ppermute | solution.py:23
  116.6 405.4 %collective-permute-start.47 = (f32[32,1,64]{2,1,0:T(1,128)}, f32[32,1,64]{2,1,0:T(1,128)}, u32[]{:S(2)}, u32[]{:S(2)}) collective-permute-start(f32[32,1,64]{2,1,0:T(1,128)} %get-tuple-element.1761), channel_id=1, source_target_pairs={{2,0},{4,2},{6,4},{8,6},{10,8},{12,10},{14,12},{3,1},{5,3},{7,5},{... | collective-permute-start | bytes 24584 | tf_op jit(solution)/shard_map/ppermute | solution.py:25
  129.0 176.1 %collective-permute-start.36 = (f32[10,1,64]{2,1,0:T(1,128)S(1)}, f32[10,1,64]{2,1,0:T(1,128)S(1)}, u32[]{:S(2)}, u32[]{:S(2)}) collective-permute-start(f32[10,1,64]{2,1,0:T(1,128)S(1)} %get-tuple-element.1769), channel_id=1, source_target_pairs={{0,2},{2,4},{4,6},{6,8},{8,10},{10,12},{12,14},{1,3},{3,5},{5,7},{... | collective-permute-start | bytes 7688 | tf_op jit(solution)/shard_map/ppermute | solution.py:23
  144.4 9.1 collective-permute-start.10
  151.6 8.0 collective-permute-start.11
  188.9 8.0 collective-permute-start.11
  199.6 9.5 collective-permute-start.12
  230.4 8.0 collective-permute-start.11
  241.1 9.3 collective-permute-start.12
  270.5 8.0 collective-permute-start.11
  281.2 9.3 collective-permute-start.12
  310.2 10.4 collective-permute-start.42
  313.6 13.1 %collective-permute-start.43 = (f32[18,1,128]{2,1,0:T(1,128)S(1)}, f32[18,1,128]{2,1,0:T(1,128)S(1)}, u32[]{:S(2)}, u32[]{:S(2)}) collective-permute-start(f32[18,1,128]{2,1,0:T(1,128)S(1)} %get-tuple-element.1751), channel_id=1, source_target_pairs={{2,0},{4,2},{6,4},{8,6},{10,8},{12,10},{14,12},{3,1},{5,3},{7,5},{... | collective-permute-start | bytes 27656 | tf_op jit(solution)/shard_map/ppermute | solution.py:25
  319.3 14.5 %collective-permute-start.38 = (f32[10,34,1]{2,1,0:T(8,128)S(1)}, f32[10,34,1]{2,1,0:T(8,128)}, u32[]{:S(2)}, u32[]{:S(2)}) collective-permute-start(f32[10,34,1]{2,1,0:T(8,128)S(1)} %get-tuple-element.1765), channel_id=1, source_target_pairs={{0,1},{2,3},{4,5},{6,7},{8,9},{10,11},{12,13},{14,15},{16,17},{18,... | collective-permute-start | bytes 4088 | tf_op jit(solution)/shard_map/ppermute | solution.py:23
  320.6 17.0 %collective-permute-start.39 = (f32[10,34,1]{2,1,0:T(8,128)S(1)}, f32[10,34,1]{2,1,0:T(8,128)}, u32[]{:S(2)}, u32[]{:S(2)}) collective-permute-start(f32[10,34,1]{2,1,0:T(8,128)S(1)} %get-tuple-element.1764), channel_id=1, source_target_pairs={{1,0},{3,2},{5,4},{7,6},{9,8},{11,10},{13,12},{15,14},{17,16},{19,... | collective-permute-start | bytes 4088 | tf_op jit(solution)/shard_map/ppermute | solution.py:25
  333.9 8.2 collective-permute-start.45
  419.1 8.3 collective-permute-start.4
  452.7 10.6 collective-permute-start.4
  487.7 10.6 collective-permute-start.4
  513.1 10.1 collective-permute-start.50
  515.0 8.2 collective-permute-start.51
  523.4 9.5 collective-permute-start.52
  524.7 8.1 collective-permute-start.53
  568.7 12.1 %collective-permute-start.6 = (f32[32,1,64]{2,1,0:T(1,128)}, f32[32,1,64]{2,1,0:T(1,128)S(1)}, u32[]{:S(2)}, u32[]{:S(2)}) collective-permute-start(f32[32,1,64]{2,1,0:T(1,128)} %get-tuple-element.2240), channel_id=1, source_target_pairs={{2,0},{4,2},{6,4},{8,6},{10,8},{12,10},{14,12},{3,1},{5,3},{7,5},{... | collective-permute-start | bytes 24584 | tf_op jit(solution)/shard_map/while/body/eval_jaxpr/ppermute | solution.py:25
  576.2 8.4 collective-permute-start.7
  594.3 8.4 collective-permute-start.7
  612.3 8.4 collective-permute-start.7
  626.7 46.5 %collective-permute-start.54 = (f32[32,1,64]{2,1,0:T(1,128)S(1)}, f32[32,1,64]{2,1,0:T(1,128)S(1)}, u32[]{:S(2)}, u32[]{:S(2)}) collective-permute-start(f32[32,1,64]{2,1,0:T(1,128)S(1)} %get-tuple-element.1758), channel_id=1, source_target_pairs={{0,2},{2,4},{4,6},{6,8},{8,10},{10,12},{12,14},{1,3},{3,5},{5,7},{... | collective-permute-start | bytes 24584 | tf_op jit(solution)/shard_map/ppermute | solution.py:23
  628.6 44.6 %collective-permute-start.55 = (f32[32,1,64]{2,1,0:T(1,128)S(1)}, f32[32,1,64]{2,1,0:T(1,128)S(1)}, u32[]{:S(2)}, u32[]{:S(2)}) collective-permute-start(f32[32,1,64]{2,1,0:T(1,128)S(1)} %get-tuple-element.1759), channel_id=1, source_target_pairs={{2,0},{4,2},{6,4},{8,6},{10,8},{12,10},{14,12},{3,1},{5,3},{7,5},{... | collective-permute-start | bytes 24584 | tf_op jit(solution)/shard_map/ppermute | solution.py:25
  787.2 8.4 collective-permute-start.15
  805.1 8.4 collective-permute-start.15
  823.2 8.4 collective-permute-start.15
  841.2 8.4 collective-permute-start.15
  874.7 26.1 %collective-permute-start.20 = (f32[10,34,1]{2,1,0:T(8,128)S(1)}, f32[10,34,1]{2,1,0:T(8,128)}, u32[]{:S(2)}, u32[]{:S(2)}) collective-permute-start(f32[10,34,1]{2,1,0:T(8,128)S(1)} %get-tuple-element.2306), channel_id=1, source_target_pairs={{1,0},{3,2},{5,4},{7,6},{9,8},{11,10},{13,12},{15,14},{17,16},{19,... | collective-permute-start | bytes 4088 | tf_op jit(solution)/shard_map/while/body/eval_jaxpr/ppermute | solution.py:25
  925.1 10.5 collective-permute-start.20
  959.8 10.5 collective-permute-start.20
  992.7 10.5 collective-permute-start.20
  1025.5 8.0 collective-permute-start.25
  1036.2 11.2 collective-permute-start.26
  1077.7 10.5 collective-permute-start.26
  1118.5 10.5 collective-permute-start.26
  1159.4 10.5 collective-permute-start.26
  (133 other events, 1623.8 us)
where the time goes:
time: 1190 us; the launch traced here: 1180 us
  starting transfers between devices  414 us (35%)
  local copies, waits for them, and re-layouts  286 us (24%)
  other arithmetic  215 us (18%)
  waiting for transfers between devices  158 us (13%)
  blocking collectives  103 us (9%)
    ppermute x66, starting transfers between devices, padded_2(): lax.ppermute(head, axis, [((i + 1) % count, i) for i in range(ends)])  241 us
    ppermute x66, starting transfers between devices, padded_2(): lax.ppermute(tail, axis, [(i, (i + 1) % count) for i in range(ends)])  173 us
    add x29, other arithmetic, sweep_once(): return ((current + update, update), None)  135 us
    ppermute x66, waiting for transfers between devices, padded_2(): lax.ppermute(tail, axis, [(i, (i + 1) % count) for i in range(ends)])  97.8 us
    reshape x4, local copies, waits for them, and re-layouts, restrict_cells(): blocks = values.reshape(size_x // 2, 2, size_y // 2, 2, size_z // 2, 2)  86.9 us
    ppermute x66, waiting for transfers between devices, padded_2(): lax.ppermute(head, axis, [((i + 1) % count, i) for i in range(ends)])  60.2 us
    dynamic_slice x58, local copies, waits for them, and re-layouts, smooth(): lax.scan(sweep_once, (values, direction), (keep_weights, new_weights))  59.5 us
    reduce_sum x6, other arithmetic, restrict_cells(): return jnp.mean(blocks, axis=(1, 3, 5))  38.3 us
  transfers between devices with their start and end apart: 132, of which 39 were waited for; matrix products, arithmetic and copies ran while one was open for 24% of the time, Pallas kernels for 0%

commit v1 on v0

v1 whole, which is shorter than its diff:
```python
import jax
import jax.numpy as jnp
from jax import lax
from jax.experimental import pallas as pl
from jax.experimental.pallas import tpu as pltpu
from jax.sharding import PartitionSpec as P

DEGREE = 4
BOTTOM = 8
SMOOTH_LOW = 0.25
SMOOTH_HIGH = 2.0
BOTTOM_LOW = 0.05

F32 = jnp.float32
MESH = pl.DeviceIdType.MESH
NP = 16
NJ = 8


def chebyshev_steps(sweeps, low_end, high_end):
    center = 0.5 * (high_end + low_end)
    radius = 0.5 * (high_end - low_end)
    sigma_ratio = center / radius
    rho_old = 1.0 / sigma_ratio
    steps_out = [(0.0, 1.0 / center)]
    for sweep_index in range(1, sweeps):
        rho_new = 1.0 / (2.0 * sigma_ratio - rho_old)
        steps_out.append((rho_new * rho_old, 2.0 * rho_new / radius))
        rho_old = rho_new
    return steps_out


FINE_STEPS = chebyshev_steps(DEGREE, SMOOTH_LOW, SMOOTH_HIGH)
BOTTOM_STEPS = chebyshev_steps(BOTTOM, BOTTOM_LOW, SMOOTH_HIGH)


def loop(low, high, body):
    def step(index, carry):
        body(index)
        return carry

    lax.fori_loop(low, high, step, 0)


def lanes(shape):
    return lax.broadcasted_iota(jnp.int32, shape, len(shape) - 1)


class Moves:
    def __init__(self, place, ref, send, recv, dirs):
        self.place, self.ref, self.send, self.recv, self.dirs = place, ref, send, recv, dirs

    def copy(self, at):
        p, j = self.place
        dp, dj, src, dst = self.dirs[at]
        to = p + dp
        return pltpu.make_async_remote_copy(
            src_ref=self.ref.at[src],
            dst_ref=self.ref.at[dst],
            send_sem=self.send.at[at],
            recv_sem=self.recv.at[at],
            device_id=(to // 2, j + dj, to % 2),
            device_id_type=MESH,
        )

    def each(self, sign, act):
        p, j = self.place
        for at, (dp, dj, src, dst) in enumerate(self.dirs):
            ok = None
            for value, count, shift in ((p, NP, sign * dp), (j, NJ, sign * dj)):
                if shift > 0:
                    good = value < count - shift
                elif shift < 0:
                    good = value >= -shift
                else:
                    continue
                ok = good if ok is None else jnp.logical_and(ok, good)

            @pl.when(ok)
            def _():
                act(self.copy(at))

    def start(self):
        self.each(1, lambda c: c.start())

    def arrive(self):
        self.each(-1, lambda c: c.wait_recv())

    def drain(self):
        self.each(1, lambda c: c.wait_send())


def block_dirs(planes, first, halo, row, rows, dps, djs, wide, mid=()):
    out = []
    for dj in djs:
        for dp in dps:
            if dp == 0 and dj == 0:
                continue
            if dp > 0:
                x0 = max(0, planes * dp - halo)
                count = planes - x0
            elif dp < 0:
                x0 = 0
                count = min(planes, planes + halo + planes * dp)
            else:
                x0, count = 0, planes
            if dj == 0:
                low, size = (row - 8, rows + 16) if wide else (row, rows)
                to = low
            elif dj > 0:
                low, size, to = row + rows - 8, 8, row - 8
            else:
                low, size, to = row, 8, row + rows
            a = first + x0
            src = (pl.ds(a, count),) + mid + (pl.ds(low, size),)
            dst = (pl.ds(a - planes * dp, count),) + mid + (pl.ds(to, size),)
            out.append((dp, dj, src, dst))
    return out


def line(ref, start):
    return ref[pl.ds(start, 8, stride=2)]


def kernel(
    iterate, right_side, diffusion, out,
    sv, sc, sg, perm, back, tmp,
    va, vb, dd, gg, jj, di, wx, wl, wr, wz, wm, cc, pre, obuf,
    s1, c1, k1, va1, vb1, d1, j1, i1, wx1, wl1, wr1, zl1, zr1,
    s2, c2, k2, va2, vb2, d2, j2, i2, wx2, wl2, wr2, zl2, zr2,
    s3, c3, va3, vb3, d3, j3, i3, wx3, wl3, wr3, zl3, zr3,
    x_send, x_recv, self_sem,
    s1_send, s1_recv, s2_send, s2_recv,
    y_send, y_recv, h_send, h_recv, g_send, g_recv, o_send, o_recv,
):
    i = lax.axis_index("gx")
    j = lax.axis_index("gy")
    k = lax.axis_index("gz")
    p = 2 * i + k
    place = (p, j)

    barrier = pltpu.get_barrier_semaphore()

    def greet(to, tj):
        pl.semaphore_signal(
            barrier, inc=1, device_id=(to // 2, tj, to % 2), device_id_type=MESH
        )

    loop(1, NP, lambda q: greet((p + q) % NP, j))
    count = NP - 1
    for dj in (-1, 1, -2, 2):
        okj = jnp.logical_and(j + dj >= 0, j + dj < NJ)
        for dp in range(-3, 4) if abs(dj) == 1 else (0,):
            ok = jnp.logical_and(okj, jnp.logical_and(p + dp >= 0, p + dp < NP))
            count = count + ok.astype(jnp.int32)

            @pl.when(ok)
            def _():
                greet(p + dp, j + dj)

    pl.semaphore_wait(barrier, count)

    def fine_moves(at, src, dst, halo):
        n = 8 + halo
        sends = []

        def copy(slot_s, slot_r, x0, nx, a0, low, size, to, zh, dev):
            return pltpu.make_async_remote_copy(
                src_ref=src.at[pl.ds(x0, nx), pl.ds(low, size)],
                dst_ref=dst.at[pl.ds(a0, nx), zh, pl.ds(to, size)],
                send_sem=x_send.at[at, slot_s],
                recv_sem=x_recv.at[at, slot_r],
                device_id=dev,
                device_id_type=MESH,
            )

        mine = pltpu.make_async_copy(
            src.at[pl.ds(k * (8 - halo), n)],
            dst.at[pl.ds(5 - halo * k, n), k, pl.ds(8, 64)],
            self_sem.at[at],
        )
        other = 1 - k
        sends.append((None, copy(0, 0, other * (8 - halo), n, 5 - halo * other, 0, 64, 8, k, (i, j, other))))
        rows = [(0, 0, 64, 8), (1, 56, 8, 0), (-1, 0, 8, 72)]
        for dj, low, size, to in rows:
            okj = jnp.logical_and(j + dj >= 0, j + dj < NJ)
            turn = {0: 0, 1: 1, -1: 2}[dj]
            up = jnp.logical_and(i < 7, okj)
            down = jnp.logical_and(i > 0, okj)
            slot = 1 + 2 * turn + k
            sends.append((up, copy(1 + 2 * turn, slot, 16 - halo, halo, 5 - halo, low, size, to, k, (i + 1, j + dj, 0))))
            sends.append((down, copy(2 + 2 * turn, slot, 0, halo, 13, low, size, to, k, (i - 1, j + dj, 1))))
            if dj != 0:
                for half in (0, 1):
                    sends.append(
                        (okj, copy(5 + 2 * turn + half, 5 + 2 * turn + k, half * (8 - halo), n, 5 - halo * half, low, size, to, k, (i, j + dj, half)))
                    )

        def start():
            mine.start()
            for ok, c in sends:
                if ok is None:
                    c.start()
                else:
                    pl.when(ok)(c.start)

        def arrive():
            mine.wait()
            copy(0, 0, 0, n, 5 - halo * k, 0, 64, 8, other, (i, j, other)).wait_recv()
            beside = jnp.logical_or(jnp.logical_and(k == 0, i > 0), jnp.logical_and(k == 1, i < 7))
            a0 = (5 - halo) * (1 - k) + 13 * k
            for dj, low, size, to in rows:
                turn = {0: 0, 1: 1, -1: 2}[dj]
                okj = jnp.logical_and(j - dj >= 0, j - dj < NJ)
                ok = jnp.logical_and(beside, okj)
                for half in (0, 1):
                    pl.when(ok)(copy(0, 1 + 2 * turn + half, 0, halo, a0, low, size, to, half, (i, j, other)).wait_recv)
                    if dj != 0:
                        pl.when(okj)(copy(0, 5 + 2 * turn + half, 0, n, 5 - halo * k, low, size, to, half, (i, j, other)).wait_recv)

        def drain():
            for ok, c in sends:
                if ok is None:
                    c.wait_send()
                else:
                    pl.when(ok)(c.wait_send)

        return start, arrive, drain

    moves_c = fine_moves(0, diffusion, sc, 5)
    moves_v = fine_moves(1, iterate, sv, 5)
    moves_g = fine_moves(2, right_side, sg, 4)
    moves_c[0]()
    moves_v[0]()
    moves_g[0]()

    def clear(ref, planes, low_planes, high_from, edges, own=None):
        def wipe(a):
            ref[a] = jnp.zeros(ref.shape[1:], F32)

        loop(0, low_planes, wipe)
        loop(high_from, planes, wipe)

        def wipe_rows(low, size):
            def one(a):
                if len(ref.shape) == 4:
                    ref[a, :, low:low + size] = jnp.zeros((2, size, 128), F32)
                else:
                    ref[a, low:low + size] = jnp.zeros((size, 128), F32)

            loop(*(own or (0, planes)), one)

        for test, low, size in edges:
            pl.when(test)(lambda low=low, size=size: wipe_rows(low, size))

    def outer(first, planes, per, total):
        low = jnp.clip(first - per * p, 0, planes)
        high = jnp.clip(total - per * p + first, 0, planes)
        return low, high

    low, high = outer(5, 18, 8, 128)
    for ref in (sv, sc, sg):
        clear(ref, 18, low, high, [(j == 0, 0, 8), (j == 7, 72, 8)])
    clear(pre, 18, low, high, [(j == 0, 8, 8), (j == 7, 80, 8)], (5, 13))
    low, high = outer(6, 16, 4, 64)
    for ref, own in ((s1, None), (c1, (6, 10)), (k1, (6, 10))):
        clear(ref, 16, low, high, [(j == 0, 8, 8), (j == 7, 48, 8)], own)
    low, high = outer(7, 16, 2, 32)
    for ref, own in ((s2, None), (c2, (7, 9)), (k2, (7, 9))):
        clear(ref, 16, low, high, [(j == 0, 8, 8), (j == 7, 32, 8)], own)
    for ref in (s3, c3):
        clear(ref, 18, 1, 17, [(j == 0, 8, 16), (j == 1, 8, 8), (j == 6, 40, 8), (j == 7, 32, 16)], (p + 1, p + 2))
    for ref in (va3, vb3):
        clear(ref, 18, 1, 17, [])

    row = lax.broadcasted_iota(jnp.int32, (256, 256), 0)
    col = lax.broadcasted_iota(jnp.int32, (256, 256), 1)

    def taken(of):
        return jnp.where(of < 128, 2 * of, 2 * of - 255)

    perm[...] = jnp.where(row == taken(col), 1.0, 0.0).astype(jnp.bfloat16)
    back[...] = jnp.where(col == taken(row), 1.0, 0.0).astype(jnp.bfloat16)

    def shuffle(left, right, matrix):
        both = jnp.concatenate([left, right], axis=1)
        high = both.astype(jnp.bfloat16)
        rest = both - high.astype(F32)
        mid = rest.astype(jnp.bfloat16)
        low = (rest - mid.astype(F32)).astype(jnp.bfloat16)
        m = matrix[...]
        res = jnp.dot(high, m, preferred_element_type=F32)
        res = res + jnp.dot(mid, m, preferred_element_type=F32)
        res = res + jnp.dot(low, m, preferred_element_type=F32)
        return res[:, :128], res[:, 128:]

    def split(src, dst, low, high):
        def one(a):
            even, odd = shuffle(src[a, 0], src[a, 1], perm)
            dst[a, 0, 4:84] = even
            dst[a, 1, 4:84] = odd

        loop(low, high, one)

    def fold_rows(at):
        return line(tmp, 16 * at) + line(tmp, 16 * at + 1)

    def fold_lanes(value, step):
        even = (lanes(value.shape) // step) % 2 == 0
        return value + jnp.where(even, pltpu.roll(value, 128 - step, 1), pltpu.roll(value, step, 1))

    moves_c[1]()
    split(sc, cc, 0, 18)

    def coarsen_c(m):
        a = 5 + 2 * m
        w = slice(12, 76)
        tmp[...] = (cc[a, 0, w] + cc[a, 1, w]) + (cc[a + 1, 0, w] + cc[a + 1, 1, w])
        for t in range(4):
            c1[6 + m, 16 + 8 * t:24 + 8 * t] = 0.125 * fold_rows(t)

    loop(0, 4, coarsen_c)
    for m in range(2):
        tmp[0:32] = c1[6 + 2 * m, 16:48] + c1[7 + 2 * m, 16:48]
        for t in range(2):
            c2[7 + m, 16 + 8 * t:24 + 8 * t] = 0.125 * fold_lanes(fold_rows(t), 1)
    tmp[0:16] = c2[7, 16:32] + c2[8, 16:32]
    c3[p + 1, 24:32] = 0.125 * fold_lanes(fold_rows(0), 2)

    def y_moves(at, ref, planes, first, row, rows, mid=()):
        dirs = block_dirs(planes, first, 0, row, rows, (0,), (-1, 1), False, mid)
        return Moves(place, ref, y_send.at[at], y_recv.at[at], dirs)

    def h_moves(at, ref, planes, first, halo, row, rows, reach, mid=()):
        dps = [d for d in range(-reach, reach + 1) if d != 0]
        dirs = block_dirs(planes, first, halo, row, rows, dps, (0,), True, mid)
        return Moves(place, ref, h_send.at[at], h_recv.at[at], dirs)

    def column_moves(at, ref):
        here = (p + 1, pl.ds(24, 8))
        dirs = [(0, dj, here, (p + 1, pl.ds(24 - 8 * dj, 8))) for dj in (-2, -1, 1, 2)]
        return Moves(place, ref, y_send.at[at], y_recv.at[at], dirs)

    class Around:
        def __init__(self, at, ref):
            self.at, self.ref = at, ref

        def copy(self, q, plane):
            to = (p + q) % NP
            return pltpu.make_async_remote_copy(
                src_ref=self.ref.at[plane, pl.ds(8, 40)],
                dst_ref=self.ref.at[plane, pl.ds(8, 40)],
                send_sem=g_send.at[self.at, q],
                recv_sem=g_recv.at[self.at, q],
                device_id=(to // 2, j, to % 2),
                device_id_type=MESH,
            )

        def start(self):
            loop(1, NP, lambda q: self.copy(q, p + 1).start())

        def arrive(self):
            loop(1, NP, lambda q: self.copy(q, (p - q + NP) % NP + 1).wait_recv())

        def drain(self):
            loop(1, NP, lambda q: self.copy(q, p + 1).wait_send())

    y_c1 = y_moves(0, c1, 4, 6, 16, 32)
    y_c2 = y_moves(1, c2, 2, 7, 16, 16)
    y_c3 = column_moves(2, c3)
    h_c1 = h_moves(0, c1, 4, 6, 6, 16, 32, 2)
    h_c2 = h_moves(1, c2, 2, 7, 7, 16, 16, 4)
    h_c3 = Around(0, c3)
    y_pre = y_moves(3, pre, 8, 5, 16, 64, (slice(None),))
    h_pre = h_moves(2, pre, 8, 5, 4, 16, 64, 1, (slice(None),))
    y_k1 = y_moves(4, k1, 4, 6, 16, 32)
    h_k1 = h_moves(3, k1, 4, 6, 6, 16, 32, 2)
    y_k2 = y_moves(5, k2, 2, 7, 16, 16)
    h_k2 = h_moves(4, k2, 2, 7, 7, 16, 16, 4)
    y_s3 = column_moves(6, s3)
    h_s3 = Around(1, s3)
    m_s1 = Moves(place, s1, s1_send, s1_recv, block_dirs(4, 6, 5, 16, 32, range(-2, 3), (0, -1, 1), False))
    m_s2 = Moves(place, s2, s2_send, s2_recv, block_dirs(2, 7, 6, 16, 16, range(-3, 4), (0, -1, 1), False))

    y_c1.start()
    y_c2.start()
    y_c3.start()

    wide = slice(8, 80)
    lane = lanes((72, 128))

    def weights(a):
        wx[a, :, wide] = 0.5 * (cc[a, :, wide] + cc[a + 1, :, wide])

    def fine_setup(a):
        weights(a)
        even = cc[a, 0, wide]
        odd = cc[a, 1, wide]
        left = jnp.where(lane == 0, 0.0, pltpu.roll(odd, 1, 1))
        right = jnp.where(lane == 127, 0.0, pltpu.roll(even, 127, 1))
        wm[a, wide] = 0.5 * (even + odd)
        wz[a, 0, wide] = jnp.where(lane == 0, 0.0, 0.5 * (even + left))
        wz[a, 1, wide] = jnp.where(lane == 127, 0.0, 0.5 * (odd + right))
        for h, mid, zs in ((0, even, left + odd), (1, odd, even + right)):
            yl = cc[a, h, 7:79]
            yr = cc[a, h, 9:81]
            wl[a, h, wide] = 0.5 * (mid + yl)
            wr[a, h, wide] = 0.5 * (mid + yr)
            diag = 0.5 * (6.0 * mid + (cc[a - 1, h, wide] + cc[a + 1, h, wide]) + (yl + yr) + zs)
            di[a, h, wide] = diag
            jj[a, h, wide] = jnp.where(mid > 0.0, 1.0 / diag, 0.0)

    weights(0)
    loop(1, 17, fine_setup)

    moves_v[1]()
    split(sv, va, 0, 18)
    moves_g[1]()
    split(sg, gg, 1, 17)

    def fine_sum(src, a, low, high):
        w = slice(low, high)
        even = src[a, 0, w]
        odd = src[a, 1, w]
        res = []
        for h, mid in ((0, even), (1, odd)):
            total = gg[a, h, w] + wx[a - 1, h, w] * src[a - 1, h, w] + wx[a, h, w] * src[a + 1, h, w]
            total = total + wl[a, h, w] * src[a, h, low - 1:high - 1] + wr[a, h, w] * src[a, h, low + 1:high + 1]
            if h == 0:
                total = total + wz[a, 0, w] * pltpu.roll(odd, 1, 1) + wm[a, w] * odd
            else:
                total = total + wm[a, w] * even + wz[a, 1, w] * pltpu.roll(even, 127, 1)
            res.append((mid, total))
        return res

    def fine_sweep(src, dst, step, halo):
        keep, new = FINE_STEPS[step]

        def one(a):
            for h, (mid, total) in enumerate(fine_sum(src, a, 8, 80)):
                move = new * (jj[a, h, wide] * total - mid)
                if step > 0:
                    move = move + keep * dd[a, h, wide]
                dd[a, h, wide] = move
                dst[a, h, wide] = mid + move

        loop(5 - halo, 13 + halo, one)

    fine_sweep(va, vb, 0, 4)
    fine_sweep(vb, va, 1, 3)
    y_c1.arrive()
    y_c2.arrive()
    y_c3.arrive()
    h_c1.start()
    h_c2.start()
    h_c3.start()
    fine_sweep(va, vb, 2, 2)
    fine_sweep(vb, va, 3, 1)

    def fine_residual(m):
        w = slice(12, 76)
        total = None
        for a in (5 + 2 * m, 6 + 2 * m):
            for h, (mid, acc) in enumerate(fine_sum(va, a, 12, 76)):
                part = acc - di[a, h, w] * mid
                total = part if total is None else total + part
        tmp[...] = total
        for t in range(4):
            s1[6 + m, 16 + 8 * t:24 + 8 * t] = 0.125 * fold_rows(t)

    loop(0, 4, fine_residual)
    m_s1.start()

    def keep_fine(a):
        pre[a, :, 16:80] = va[a, :, 12:76]

    loop(5, 13, keep_fine)
    y_pre.start()

    def setup(c, jn, dn, wxn, wln, wrn, zln, zrn, planes, rows, step, scale):
        low, high = planes
        r0, r1 = rows
        w = slice(r0, r1)
        spot = lanes((r1 - r0, 128))
        half = 0.5 * scale

        def across(a):
            wxn[a, w] = half * (c[a, w] + c[a + 1, w])

        def one(a):
            across(a)
            mid = c[a, w]
            left = jnp.where(spot < step, 0.0, pltpu.roll(mid, step, 1))
            right = jnp.where(spot >= 128 - step, 0.0, pltpu.roll(mid, 128 - step, 1))
            yl = c[a, r0 - 1:r1 - 1]
            yr = c[a, r0 + 1:r1 + 1]
            wln[a, w] = half * (mid + yl)
            wrn[a, w] = half * (mid + yr)
            zln[a, w] = jnp.where(spot < step, 0.0, half * (mid + left))
            zrn[a, w] = jnp.where(spot >= 128 - step, 0.0, half * (mid + right))
            diag = half * (6.0 * mid + (c[a - 1, w] + c[a + 1, w]) + (yl + yr) + (left + right))
            dn[a, w] = diag
            jn[a, w] = jnp.where(mid > 0.0, 1.0 / diag, 0.0)

        across(low - 1)
        loop(low, high, one)

    def gather_sum(src, a, g, wxn, wln, wrn, zln, zrn, rows, step):
        r0, r1 = rows
        w = slice(r0, r1)
        mid = src[a, w]
        total = g[a, w] + wxn[a - 1, w] * src[a - 1, w] + wxn[a, w] * src[a + 1, w]
        total = total + wln[a, w] * src[a, r0 - 1:r1 - 1] + wrn[a, w] * src[a, r0 + 1:r1 + 1]
        total = total + zln[a, w] * pltpu.roll(mid, step, 1) + zrn[a, w] * pltpu.roll(mid, 128 - step, 1)
        return mid, total

    def sweep(src, dst, d, jn, ws, planes, rows, step, pair):
        keep, new = pair
        w = slice(*rows)

        def one(a):
            mid, total = gather_sum(src, a, *ws, rows, step)
            move = new * (jn[a, w] * total - mid)
            if keep != 0.0:
                move = move + keep * d[a, w]
            d[a, w] = move
            dst[a, w] = mid + move

        loop(planes[0], planes[1], one)

    def first(dst, d, g, jn, planes, rows, new):
        w = slice(*rows)

        def one(a):
            move = new * (jn[a, w] * g[a, w])
            d[a, w] = move
            dst[a, w] = move

        loop(planes[0], planes[1], one)

    ws1 = (s1, wx1, wl1, wr1, zl1, zr1)
    ws2 = (s2, wx2, wl2, wr2, zl2, zr2)
    ws3 = (s3, wx3, wl3, wr3, zl3, zr3)
    rows1, rows2, rows3 = (8, 56), (8, 40), (8, 48)

    h_c1.arrive()
    setup(c1, j1, i1, wx1, wl1, wr1, zl1, zr1, (1, 15), rows1, 1, 0.25)
    h_c2.arrive()
    setup(c2, j2, i2, wx2, wl2, wr2, zl2, zr2, (1, 15), rows2, 2, 0.0625)
    h_c3.arrive()
    setup(c3, j3, i3, wx3, wl3, wr3, zl3, zr3, (1, 17), rows3, 4, 0.015625)

    m_s1.arrive()
    first(va1, d1, s1, j1, (2, 14), rows1, FINE_STEPS[0][1])
    sweep(va1, vb1, d1, j1, ws1, (3, 13), rows1, 1, FINE_STEPS[1])
    sweep(vb1, va1, d1, j1, ws1, (4, 12), rows1, 1, FINE_STEPS[2])
    sweep(va1, vb1, d1, j1, ws1, (5, 11), rows1, 1, FINE_STEPS[3])

    def residual(src, a, ws, dn, rows, step):
        mid, total = gather_sum(src, a, *ws, rows, step)
        return total - dn[a, slice(*rows)] * mid

    for m in range(2):
        a = 6 + 2 * m
        tmp[0:32] = residual(vb1, a, ws1, i1, (16, 48), 1) + residual(vb1, a + 1, ws1, i1, (16, 48), 1)
        for t in range(2):
            s2[7 + m, 16 + 8 * t:24 + 8 * t] = 0.125 * fold_lanes(fold_rows(t), 1)
    m_s2.start()
    k1[6:10, 16:48] = vb1[6:10, 16:48]
    y_k1.start()
    y_pre.arrive()
    h_pre.start()

    m_s2.arrive()
    first(va2, d2, s2, j2, (3, 13), rows2, FINE_STEPS[0][1])
    sweep(va2, vb2, d2, j2, ws2, (4, 12), rows2, 2, FINE_STEPS[1])
    sweep(vb2, va2, d2, j2, ws2, (5, 11), rows2, 2, FINE_STEPS[2])
    sweep(va2, vb2, d2, j2, ws2, (6, 10), rows2, 2, FINE_STEPS[3])
    tmp[0:16] = residual(vb2, 7, ws2, i2, (16, 32), 2) + residual(vb2, 8, ws2, i2, (16, 32), 2)
    s3[p + 1, 24:32] = 0.125 * fold_lanes(fold_rows(0), 2)
    y_s3.start()
    k2[7:9, 16:32] = vb2[7:9, 16:32]
    y_k2.start()
    y_k1.arrive()
    h_k1.start()
    y_s3.arrive()
    h_s3.start()
    y_k2.arrive()
    h_k2.start()

    h_s3.arrive()
    first(va3, d3, s3, j3, (1, 17), rows3, BOTTOM_STEPS[0][1])
    here, there = va3, vb3
    for at in range(1, BOTTOM):
        halo = BOTTOM + 3 - at
        planes = (jnp.maximum(1, p + 1 - halo), jnp.minimum(17, p + 2 + halo))
        sweep(here, there, d3, j3, ws3, planes, rows3 if halo > 8 else (16, 40), 4, BOTTOM_STEPS[at])
        here, there = there, here

    h_k2.arrive()

    def finish2(a):
        up = jnp.clip(p - 3 + (a + 1) // 2, 0, 17)
        for t in range(2):
            e = here[up, 20 + 8 * t:28 + 8 * t]
            for odd in range(2):
                at = pl.ds(8 + 16 * t + odd, 8, stride=2)
                va2[a, at] = k2[a, at] + e

    loop(0, 16, finish2)
    sweep(va2, vb2, d2, j2, ws2, (1, 15), rows2, 2, FINE_STEPS[0])
    sweep(vb2, va2, d2, j2, ws2, (2, 14), rows2, 2, FINE_STEPS[1])
    sweep(va2, vb2, d2, j2, ws2, (3, 13), rows2, 2, FINE_STEPS[2])
    sweep(vb2, va2, d2, j2, ws2, (4, 12), rows2, 2, FINE_STEPS[3])

    h_k1.arrive()

    def finish1(a):
        up = 4 + a // 2
        for t in range(3):
            e = va2[up, 12 + 8 * t:20 + 8 * t]
            for odd in range(2):
                at = pl.ds(8 + 16 * t + odd, 8, stride=2)
                va1[a, at] = k1[a, at] + e

    loop(0, 16, finish1)
    sweep(va1, vb1, d1, j1, ws1, (1, 15), rows1, 1, FINE_STEPS[0])
    sweep(vb1, va1, d1, j1, ws1, (2, 14), rows1, 1, FINE_STEPS[1])
    sweep(va1, vb1, d1, j1, ws1, (3, 13), rows1, 1, FINE_STEPS[2])
    sweep(vb1, va1, d1, j1, ws1, (4, 12), rows1, 1, FINE_STEPS[3])

    h_pre.arrive()

    def finish0(m):
        for t in range(5):
            e = va1[4 + m, 14 + 8 * t:22 + 8 * t]
            for x in range(2):
                a = 1 + 2 * m + x
                for h in range(2):
                    for odd in range(2):
                        got = pre[a, h, pl.ds(12 + 16 * t + odd, 8, stride=2)]
                        va[a, h, pl.ds(8 + 16 * t + odd, 8, stride=2)] = got + e

    loop(0, 8, finish0)
    fine_sweep(va, vb, 0, 3)
    fine_sweep(vb, va, 1, 2)
    fine_sweep(va, vb, 2, 1)
    fine_sweep(vb, va, 3, 0)

    def join(x):
        left, right = shuffle(va[5 + x, 0, 12:76], va[5 + x, 1, 12:76], back)
        obuf[0, x] = left
        obuf[1, x] = right

    loop(0, 8, join)
    give = pltpu.make_async_remote_copy(
        src_ref=obuf.at[1 - k],
        dst_ref=out.at[pl.ds(8 * k, 8)],
        send_sem=o_send,
        recv_sem=o_recv,
        device_id=(i, j, 1 - k),
        device_id_type=MESH,
    )
    give.start()
    out[pl.ds(8 * k, 8)] = obuf[k]
    give.wait_send()
    pltpu.make_async_remote_copy(
        src_ref=obuf.at[k],
        dst_ref=out.at[pl.ds(8 * (1 - k), 8)],
        send_sem=o_send,
        recv_sem=o_recv,
        device_id=(i, j, 1 - k),
        device_id_type=MESH,
    ).wait_recv()

    for moves in (moves_c, moves_v, moves_g):
        moves[2]()
    for moves in (y_c1, y_c2, y_c3, h_c1, h_c2, h_c3, m_s1, y_pre, h_pre, m_s2, y_k1, h_k1, y_s3, h_s3, y_k2, h_k2):
        moves.drain()


def on_device(iterate, right_side, diffusion):
    def buf(*shape):
        return pltpu.VMEM(shape, F32)

    fine = [buf(18, 2, 88, 128)] * 10
    scratch = [buf(18, 2, 80, 128)] * 3
    scratch += [pltpu.VMEM((256, 256), jnp.bfloat16)] * 2 + [buf(64, 128)]
    scratch += fine + [buf(18, 88, 128), buf(18, 2, 88, 128), buf(18, 2, 96, 128), buf(2, 8, 64, 128)]
    scratch += [buf(16, 64, 128)] * 13
    scratch += [buf(16, 48, 128)] * 13
    scratch += [buf(18, 56, 128)] * 12
    dma = pltpu.SemaphoreType.DMA
    scratch += [dma((3, 11)), dma((3, 11)), dma((3,))]
    scratch += [dma((14,)), dma((14,)), dma((20,)), dma((20,))]
    scratch += [dma((7, 4)), dma((7, 4)), dma((5, 8)), dma((5, 8)), dma((2, NP)), dma((2, NP)), dma, dma]
    return pl.pallas_call(
        kernel,
        out_shape=jax.ShapeDtypeStruct((16, 64, 128), F32),
        in_specs=[pl.BlockSpec(memory_space=pl.ANY)] * 3,
        out_specs=pl.BlockSpec(memory_space=pltpu.VMEM),
        scratch_shapes=scratch,
        compiler_params=pltpu.CompilerParams(
            collective_id=0, has_side_effects=True, vmem_limit_bytes=60 * 2**20
        ),
        cost_estimate=pl.CostEstimate(flops=10**8, bytes_accessed=2 * 10**6, transcendentals=0),
        name="vcycle",
    )(iterate, right_side, diffusion)


def solution(mesh):
    placed = (P("gx", "gy", "gz"), P("gx", "gy", "gz"), P("gx", "gy", "gz"))
    return jax.shard_map(
        on_device, mesh=mesh, in_specs=placed, out_specs=P("gx", "gy", "gz"), check_vma=False
    )
```

time: 1190 us -> 104 us (0.09)
  the two profiles are of different devices: /device:TPU:5 before, /device:TPU:7 now
where the time goes in v1:
time: 104 us
  Pallas kernels  102 us (98%)
  local copies, waits for them, and re-layouts  1.89 us (2%)
    pallas_call x1, Pallas kernels, on_device(): pl.pallas_call(kernel, out_shape=jax.ShapeDtypeStruct((16, 64, 128), F32)...  102 us

profile of v1, /device:TPU:7, one launch (start us, length us, event | category | flops | bytes accessed | tf_op | source)
XLA Modules:
  0.0 104.0 jit_solution(654623069482935282)
XLA Ops:
  0.0 102.1 %vcycle.1 = f32[16,64,128]{2,1,0:T(8,128)} custom-call(f32[16,64,128]{2,1,0:T(8,128)} %iterate.1, f32[16,64,128]{2,1,0:T(8,128)} %right_side.1, f32[16,64,128]{2,1,0:T(8,128)} %diffusion.1), custom_call_target="tpu_custom_call" | custom-call | flops 100000000 | bytes 2000000 | tf_op jit(solution)/shard_map/vcycle/pallas_call | solution.py:697
  102.1 1.9 %copy.5 = f32[16,64,128]{2,1,0:T(8,128)} copy(f32[16,64,128]{2,1,0:T(8,128)} %vcycle.1) | data formatting | bytes 1048576

commit v2 on v1

--- a/solution.py
+++ b/solution.py
@@ -40,6 +40,18 @@
         return carry
 
     lax.fori_loop(low, high, step, 0)
+
+
+def spread(low, count, most, body):
+    runs = -(-count // most)
+    each = -(-count // runs)
+    full = count // each
+    if full > 1:
+        loop(0, full, lambda r: body(low + r * each, each))
+    elif full == 1:
+        body(low, each)
+    if count % each:
+        body(low + full * each, count % each)
 
 
 def lanes(shape):
@@ -124,8 +136,8 @@
 
 def kernel(
     iterate, right_side, diffusion, out,
-    sv, sc, sg, perm, back, tmp,
-    va, vb, dd, gg, jj, di, wx, wl, wr, wz, wm, cc, pre, obuf,
+    va, cc, gg, tmp,
+    vb, dd, jj, di, wx, wl, wr, zl, zr, pre,
     s1, c1, k1, va1, vb1, d1, j1, i1, wx1, wl1, wr1, zl1, zr1,
     s2, c2, k2, va2, vb2, d2, j2, i2, wx2, wl2, wr2, zl2, zr2,
     s3, c3, va3, vb3, d3, j3, i3, wx3, wl3, wr3, zl3, zr3,
@@ -176,12 +188,12 @@
 
         mine = pltpu.make_async_copy(
             src.at[pl.ds(k * (8 - halo), n)],
-            dst.at[pl.ds(5 - halo * k, n), k, pl.ds(8, 64)],
+            dst.at[pl.ds(5 - halo * k, n), k, pl.ds(16, 64)],
             self_sem.at[at],
         )
         other = 1 - k
-        sends.append((None, copy(0, 0, other * (8 - halo), n, 5 - halo * other, 0, 64, 8, k, (i, j, other))))
-        rows = [(0, 0, 64, 8), (1, 56, 8, 0), (-1, 0, 8, 72)]
+        sends.append((None, copy(0, 0, other * (8 - halo), n, 5 - halo * other, 0, 64, 16, k, (i, j, other))))
+        rows = [(0, 0, 64, 16), (1, 56, 8, 8), (-1, 0, 8, 80)]
         for dj, low, size, to in rows:
             okj = jnp.logical_and(j + dj >= 0, j + dj < NJ)
             turn = {0: 0, 1: 1, -1: 2}[dj]
@@ -206,7 +218,7 @@
 
         def arrive():
             mine.wait()
-            copy(0, 0, 0, n, 5 - halo * k, 0, 64, 8, other, (i, j, other)).wait_recv()
+            copy(0, 0, 0, n, 5 - halo * k, 0, 64, 16, other, (i, j, other)).wait_recv()
             beside = jnp.logical_or(jnp.logical_and(k == 0, i > 0), jnp.logical_and(k == 1, i < 7))
             a0 = (5 - halo) * (1 - k) + 13 * k
             for dj, low, size, to in rows:
@@ -227,9 +239,9 @@
 
         return start, arrive, drain
 
-    moves_c = fine_moves(0, diffusion, sc, 5)
-    moves_v = fine_moves(1, iterate, sv, 5)
-    moves_g = fine_moves(2, right_side, sg, 4)
+    moves_c = fine_moves(0, diffusion, cc, 5)
+    moves_v = fine_moves(1, iterate, va, 5)
+    moves_g = fine_moves(2, right_side, gg, 4)
     moves_c[0]()
     moves_v[0]()
     moves_g[0]()
@@ -259,8 +271,8 @@
         return low, high
 
     low, high = outer(5, 18, 8, 128)
-    for ref in (sv, sc, sg):
-        clear(ref, 18, low, high, [(j == 0, 0, 8), (j == 7, 72, 8)])
+    for ref in (va, cc, gg):
+        clear(ref, 18, low, high, [(j == 0, 8, 8), (j == 7, 80, 8)])
     clear(pre, 18, low, high, [(j == 0, 8, 8), (j == 7, 80, 8)], (5, 13))
     low, high = outer(6, 16, 4, 64)
     for ref, own in ((s1, None), (c1, (6, 10)), (k1, (6, 10))):
@@ -273,59 +285,38 @@
     for ref in (va3, vb3):
         clear(ref, 18, 1, 17, [])
 
-    row = lax.broadcasted_iota(jnp.int32, (256, 256), 0)
-    col = lax.broadcasted_iota(jnp.int32, (256, 256), 1)
-
-    def taken(of):
-        return jnp.where(of < 128, 2 * of, 2 * of - 255)
-
-    perm[...] = jnp.where(row == taken(col), 1.0, 0.0).astype(jnp.bfloat16)
-    back[...] = jnp.where(col == taken(row), 1.0, 0.0).astype(jnp.bfloat16)
-
-    def shuffle(left, right, matrix):
-        both = jnp.concatenate([left, right], axis=1)
-        high = both.astype(jnp.bfloat16)
-        rest = both - high.astype(F32)
-        mid = rest.astype(jnp.bfloat16)
-        low = (rest - mid.astype(F32)).astype(jnp.bfloat16)
-        m = matrix[...]
-        res = jnp.dot(high, m, preferred_element_type=F32)
-        res = res + jnp.dot(mid, m, preferred_element_type=F32)
-        res = res + jnp.dot(low, m, preferred_element_type=F32)
-        return res[:, :128], res[:, 128:]
-
-    def split(src, dst, low, high):
-        def one(a):
-            even, odd = shuffle(src[a, 0], src[a, 1], perm)
-            dst[a, 0, 4:84] = even
-            dst[a, 1, 4:84] = odd
-
-        loop(low, high, one)
-
-    def fold_rows(at):
-        return line(tmp, 16 * at) + line(tmp, 16 * at + 1)
+    def fold_rows(ref, at):
+        return line(ref, 16 * at) + line(ref, 16 * at + 1)
 
     def fold_lanes(value, step):
         even = (lanes(value.shape) // step) % 2 == 0
         return value + jnp.where(even, pltpu.roll(value, 128 - step, 1), pltpu.roll(value, step, 1))
 
+    def pack(halves, at):
+        low, high = (fold_lanes(fold_rows(half, at), 1) for half in halves)
+        from_lane = (2 * lanes((8, 128))) % 128
+        low = jnp.take_along_axis(low, from_lane, axis=1)
+        high = jnp.take_along_axis(high, from_lane, axis=1)
+        return 0.125 * jnp.where(lanes((8, 128)) < 64, low, high)
+
+    own = slice(16, 80)
     moves_c[1]()
-    split(sc, cc, 0, 18)
 
     def coarsen_c(m):
         a = 5 + 2 * m
-        w = slice(12, 76)
-        tmp[...] = (cc[a, 0, w] + cc[a, 1, w]) + (cc[a + 1, 0, w] + cc[a + 1, 1, w])
+        for h in range(2):
+            tmp[m, h] = cc[a, h, own] + cc[a + 1, h, own]
         for t in range(4):
-            c1[6 + m, 16 + 8 * t:24 + 8 * t] = 0.125 * fold_rows(t)
-
-    loop(0, 4, coarsen_c)
+            c1[6 + m, 16 + 8 * t:24 + 8 * t] = pack((tmp.at[m, 0], tmp.at[m, 1]), t)
+
+    for m in range(4):
+        coarsen_c(m)
     for m in range(2):
-        tmp[0:32] = c1[6 + 2 * m, 16:48] + c1[7 + 2 * m, 16:48]
+        tmp[m, 0, 0:32] = c1[6 + 2 * m, 16:48] + c1[7 + 2 * m, 16:48]
         for t in range(2):
-            c2[7 + m, 16 + 8 * t:24 + 8 * t] = 0.125 * fold_lanes(fold_rows(t), 1)
-    tmp[0:16] = c2[7, 16:32] + c2[8, 16:32]
-    c3[p + 1, 24:32] = 0.125 * fold_lanes(fold_rows(0), 2)
+            c2[7 + m, 16 + 8 * t:24 + 8 * t] = 0.125 * fold_lanes(fold_rows(tmp.at[m, 0], t), 1)
+    tmp[2, 0, 0:16] = c2[7, 16:32] + c2[8, 16:32]
+    c3[p + 1, 24:32] = 0.125 * fold_lanes(fold_rows(tmp.at[2, 0], 0), 2)
 
     def y_moves(at, ref, planes, first, row, rows, mid=()):
         dirs = block_dirs(planes, first, 0, row, rows, (0,), (-1, 1), False, mid)
@@ -386,65 +377,69 @@
     y_c2.start()
     y_c3.start()
 
-    wide = slice(8, 80)
+    wide = slice(12, 84)
     lane = lanes((72, 128))
 
-    def weights(a):
-        wx[a, :, wide] = 0.5 * (cc[a, :, wide] + cc[a + 1, :, wide])
-
-    def fine_setup(a):
-        weights(a)
-        even = cc[a, 0, wide]
-        odd = cc[a, 1, wide]
-        left = jnp.where(lane == 0, 0.0, pltpu.roll(odd, 1, 1))
-        right = jnp.where(lane == 127, 0.0, pltpu.roll(even, 127, 1))
-        wm[a, wide] = 0.5 * (even + odd)
-        wz[a, 0, wide] = jnp.where(lane == 0, 0.0, 0.5 * (even + left))
-        wz[a, 1, wide] = jnp.where(lane == 127, 0.0, 0.5 * (odd + right))
-        for h, mid, zs in ((0, even, left + odd), (1, odd, even + right)):
-            yl = cc[a, h, 7:79]
-            yr = cc[a, h, 9:81]
-            wl[a, h, wide] = 0.5 * (mid + yl)
-            wr[a, h, wide] = 0.5 * (mid + yr)
-            diag = 0.5 * (6.0 * mid + (cc[a - 1, h, wide] + cc[a + 1, h, wide]) + (yl + yr) + zs)
-            di[a, h, wide] = diag
-            jj[a, h, wide] = jnp.where(mid > 0.0, 1.0 / diag, 0.0)
-
-    weights(0)
-    loop(1, 17, fine_setup)
+    def fine_setup(low, n):
+        for a in [low + u for u in range(n)]:
+            mid = [cc[a, h, wide] for h in range(2)]
+            prev = [pltpu.roll(m, 1, 1) for m in mid]
+            foll = [pltpu.roll(m, 127, 1) for m in mid]
+            left = (jnp.where(lane == 0, 0.0, prev[0]), jnp.where(lane == 0, prev[0], prev[1]))
+            right = (jnp.where(lane == 127, foll[1], foll[0]), jnp.where(lane == 127, 0.0, foll[1]))
+            for h in range(2):
+                ahead = cc[a + 1, h, wide]
+                yl = cc[a, h, 11:83]
+                yr = cc[a, h, 13:85]
+                wx[a, h, wide] = 0.5 * (mid[h] + ahead)
+                wl[a, h, wide] = 0.5 * (mid[h] + yl)
+                wr[a, h, wide] = 0.5 * (mid[h] + yr)
+                low_edge = 0.5 * (mid[h] + left[h])
+                high_edge = 0.5 * (mid[h] + right[h])
+                zl[a, h, wide] = jnp.where(lane == 0, 0.0, low_edge) if h == 0 else low_edge
+                zr[a, h, wide] = jnp.where(lane == 127, 0.0, high_edge) if h == 1 else high_edge
+                diag = 0.5 * (6.0 * mid[h] + (cc[a - 1, h, wide] + ahead) + (yl + yr) + (left[h] + right[h]))
+                di[a, h, wide] = diag
+                jj[a, h, wide] = jnp.where(mid[h] > 0.0, 1.0 / diag, 0.0)
+
+    wx[0, :, wide] = 0.5 * (cc[0, :, wide] + cc[1, :, wide])
+    spread(1, 16, 2, fine_setup)
 
     moves_v[1]()
-    split(sv, va, 0, 18)
     moves_g[1]()
-    split(sg, gg, 1, 17)
-
-    def fine_sum(src, a, low, high):
-        w = slice(low, high)
-        even = src[a, 0, w]
-        odd = src[a, 1, w]
-        res = []
-        for h, mid in ((0, even), (1, odd)):
-            total = gg[a, h, w] + wx[a - 1, h, w] * src[a - 1, h, w] + wx[a, h, w] * src[a + 1, h, w]
-            total = total + wl[a, h, w] * src[a, h, low - 1:high - 1] + wr[a, h, w] * src[a, h, low + 1:high + 1]
-            if h == 0:
-                total = total + wz[a, 0, w] * pltpu.roll(odd, 1, 1) + wm[a, w] * odd
-            else:
-                total = total + wm[a, w] * even + wz[a, 1, w] * pltpu.roll(even, 127, 1)
-            res.append((mid, total))
-        return res
+
+    def fine_sum(src, low, n, r0, r1):
+        for r in range(r0, r1, 24 if (r1 - r0) % 24 == 0 else 32):
+            e = r + (24 if (r1 - r0) % 24 == 0 else 32)
+            w = slice(r, e)
+            spot = lanes((e - r, 128))
+            v = [[src[low + u, h, w] for h in range(2)] for u in range(-1, n + 1)]
+            x = [[wx[low + u, h, w] for h in range(2)] for u in range(-1, n)]
+            for u in range(n):
+                a = low + u
+                mid = v[u + 1]
+                prev = [pltpu.roll(m, 1, 1) for m in mid]
+                foll = [pltpu.roll(m, 127, 1) for m in mid]
+                left = (prev[0], jnp.where(spot == 0, prev[0], prev[1]))
+                right = (jnp.where(spot == 127, foll[1], foll[0]), foll[1])
+                for h in range(2):
+                    total = gg[a, h, w] + x[u][h] * v[u][h] + x[u + 1][h] * v[u + 2][h]
+                    total = total + wl[a, h, w] * src[a, h, r - 1:e - 1] + wr[a, h, w] * src[a, h, r + 1:e + 1]
+                    total = total + zl[a, h, w] * left[h] + zr[a, h, w] * right[h]
+                    yield u, a, h, w, mid[h], total
 
     def fine_sweep(src, dst, step, halo):
         keep, new = FINE_STEPS[step]
 
-        def one(a):
-            for h, (mid, total) in enumerate(fine_sum(src, a, 8, 80)):
-                move = new * (jj[a, h, wide] * total - mid)
+        def run(low, n):
+            for u, a, h, w, mid, total in fine_sum(src, low, n, 12, 84):
+                move = new * (jj[a, h, w] * total - mid)
                 if step > 0:
-                    move = move + keep * dd[a, h, wide]
-                dd[a, h, wide] = move
-                dst[a, h, wide] = mid + move
-
-        loop(5 - halo, 13 + halo, one)
+                    move = move + keep * dd[a, h, w]
+                dd[a, h, w] = move
+                dst[a, h, w] = mid + move
+
+        spread(5 - halo, 8 + 2 * halo, 4, run)
 
     fine_sweep(va, vb, 0, 4)
     fine_sweep(vb, va, 1, 3)
@@ -457,22 +452,18 @@
     fine_sweep(va, vb, 2, 2)
     fine_sweep(vb, va, 3, 1)
 
-    def fine_residual(m):
-        w = slice(12, 76)
-        total = None
-        for a in (5 + 2 * m, 6 + 2 * m):
-            for h, (mid, acc) in enumerate(fine_sum(va, a, 12, 76)):
-                part = acc - di[a, h, w] * mid
-                total = part if total is None else total + part
-        tmp[...] = total
+    for m in range(4):
+        for u, a, h, w, mid, total in fine_sum(va, 5 + 2 * m, 2, 16, 80):
+            part = total - di[a, h, w] * mid
+            spot = slice(w.start - 16, w.stop - 16)
+            tmp[m, h, spot] = part if u == 0 else tmp[m, h, spot] + part
         for t in range(4):
-            s1[6 + m, 16 + 8 * t:24 + 8 * t] = 0.125 * fold_rows(t)
-
-    loop(0, 4, fine_residual)
+            s1[6 + m, 16 + 8 * t:24 + 8 * t] = pack((tmp.at[m, 0], tmp.at[m, 1]), t)
+
     m_s1.start()
 
     def keep_fine(a):
-        pre[a, :, 16:80] = va[a, :, 12:76]
+        pre[a, :, own] = va[a, :, own]
 
     loop(5, 13, keep_fine)
     y_pre.start()
@@ -484,59 +475,60 @@
         spot = lanes((r1 - r0, 128))
         half = 0.5 * scale
 
-        def across(a):
-            wxn[a, w] = half * (c[a, w] + c[a + 1, w])
-
-        def one(a):
-            across(a)
-            mid = c[a, w]
-            left = jnp.where(spot < step, 0.0, pltpu.roll(mid, step, 1))
-            right = jnp.where(spot >= 128 - step, 0.0, pltpu.roll(mid, 128 - step, 1))
-            yl = c[a, r0 - 1:r1 - 1]
-            yr = c[a, r0 + 1:r1 + 1]
-            wln[a, w] = half * (mid + yl)
-            wrn[a, w] = half * (mid + yr)
-            zln[a, w] = jnp.where(spot < step, 0.0, half * (mid + left))
-            zrn[a, w] = jnp.where(spot >= 128 - step, 0.0, half * (mid + right))
-            diag = half * (6.0 * mid + (c[a - 1, w] + c[a + 1, w]) + (yl + yr) + (left + right))
-            dn[a, w] = diag
-            jn[a, w] = jnp.where(mid > 0.0, 1.0 / diag, 0.0)
-
-        across(low - 1)
-        loop(low, high, one)
-
-    def gather_sum(src, a, g, wxn, wln, wrn, zln, zrn, rows, step):
+        def run(first_plane, n):
+            for a in [first_plane + u for u in range(n)]:
+                mid = c[a, w]
+                ahead = c[a + 1, w]
+                left = jnp.where(spot < step, 0.0, pltpu.roll(mid, step, 1))
+                right = jnp.where(spot >= 128 - step, 0.0, pltpu.roll(mid, 128 - step, 1))
+                yl = c[a, r0 - 1:r1 - 1]
+                yr = c[a, r0 + 1:r1 + 1]
+                wxn[a, w] = half * (mid + ahead)
+                wln[a, w] = half * (mid + yl)
+                wrn[a, w] = half * (mid + yr)
+                zln[a, w] = jnp.where(spot < step, 0.0, half * (mid + left))
+                zrn[a, w] = jnp.where(spot >= 128 - step, 0.0, half * (mid + right))
+                diag = half * (6.0 * mid + (c[a - 1, w] + ahead) + (yl + yr) + (left + right))
+                dn[a, w] = diag
+                jn[a, w] = jnp.where(mid > 0.0, 1.0 / diag, 0.0)
+
+        wxn[low - 1, w] = half * (c[low - 1, w] + c[low, w])
+        spread(low, high - low, 7 if high - low == 14 else 8, run)
+
+    def gather_sum(src, low, n, g, wxn, wln, wrn, zln, zrn, rows, step):
         r0, r1 = rows
         w = slice(r0, r1)
-        mid = src[a, w]
-        total = g[a, w] + wxn[a - 1, w] * src[a - 1, w] + wxn[a, w] * src[a + 1, w]
-        total = total + wln[a, w] * src[a, r0 - 1:r1 - 1] + wrn[a, w] * src[a, r0 + 1:r1 + 1]
-        total = total + zln[a, w] * pltpu.roll(mid, step, 1) + zrn[a, w] * pltpu.roll(mid, 128 - step, 1)
-        return mid, total
+        v = [src[low + u, w] for u in range(-1, n + 1)]
+        x = [wxn[low + u, w] for u in range(-1, n)]
+        for u in range(n):
+            a = low + u
+            mid = v[u + 1]
+            total = g[a, w] + x[u] * v[u] + x[u + 1] * v[u + 2]
+            total = total + wln[a, w] * src[a, r0 - 1:r1 - 1] + wrn[a, w] * src[a, r0 + 1:r1 + 1]
+            total = total + zln[a, w] * pltpu.roll(mid, step, 1) + zrn[a, w] * pltpu.roll(mid, 128 - step, 1)
+            yield a, mid, total
 
     def sweep(src, dst, d, jn, ws, planes, rows, step, pair):
         keep, new = pair
         w = slice(*rows)
 
-        def one(a):
-            mid, total = gather_sum(src, a, *ws, rows, step)
-            move = new * (jn[a, w] * total - mid)
-            if keep != 0.0:
-                move = move + keep * d[a, w]
-            d[a, w] = move
-            dst[a, w] = mid + move
-
-        loop(planes[0], planes[1], one)
+        def run(low, n):
+            for a, mid, total in gather_sum(src, low, n, *ws, rows, step):
+                move = new * (jn[a, w] * total - mid)
+                if keep != 0.0:
+                    move = move + keep * d[a, w]
+                d[a, w] = move
+                dst[a, w] = mid + move
+
+        spread(planes[0], planes[1] - planes[0], 8, run)
 
     def first(dst, d, g, jn, planes, rows, new):
         w = slice(*rows)
 
-        def one(a):
+        for a in range(*planes):
             move = new * (jn[a, w] * g[a, w])
             d[a, w] = move
             dst[a, w] = move
-
-        loop(planes[0], planes[1], one)
 
     ws1 = (s1, wx1, wl1, wr1, zl1, zr1)
     ws2 = (s2, wx2, wl2, wr2, zl2, zr2)
@@ -556,15 +548,15 @@
     sweep(vb1, va1, d1, j1, ws1, (4, 12), rows1, 1, FINE_STEPS[2])
     sweep(va1, vb1, d1, j1, ws1, (5, 11), rows1, 1, FINE_STEPS[3])
 
-    def residual(src, a, ws, dn, rows, step):
-        mid, total = gather_sum(src, a, *ws, rows, step)
-        return total - dn[a, slice(*rows)] * mid
+    def residual(src, low, ws, dn, rows, step):
+        parts = [total - dn[a, slice(*rows)] * mid for a, mid, total in gather_sum(src, low, 2, *ws, rows, step)]
+        return parts[0] + parts[1]
 
     for m in range(2):
-        a = 6 + 2 * m
-        tmp[0:32] = residual(vb1, a, ws1, i1, (16, 48), 1) + residual(vb1, a + 1, ws1, i1, (16, 48), 1)
+        tmp[m, 0, 0:32] = residual(vb1, 6 + 2 * m, ws1, i1, (16, 48), 1)
+    for m in range(2):
         for t in range(2):
-            s2[7 + m, 16 + 8 * t:24 + 8 * t] = 0.125 * fold_lanes(fold_rows(t), 1)
+            s2[7 + m, 16 + 8 * t:24 + 8 * t] = 0.125 * fold_lanes(fold_rows(tmp.at[m, 0], t), 1)
     m_s2.start()
     k1[6:10, 16:48] = vb1[6:10, 16:48]
     y_k1.start()
@@ -576,8 +568,8 @@
     sweep(va2, vb2, d2, j2, ws2, (4, 12), rows2, 2, FINE_STEPS[1])
     sweep(vb2, va2, d2, j2, ws2, (5, 11), rows2, 2, FINE_STEPS[2])
     sweep(va2, vb2, d2, j2, ws2, (6, 10), rows2, 2, FINE_STEPS[3])
-    tmp[0:16] = residual(vb2, 7, ws2, i2, (16, 32), 2) + residual(vb2, 8, ws2, i2, (16, 32), 2)
-    s3[p + 1, 24:32] = 0.125 * fold_lanes(fold_rows(0), 2)
+    tmp[2, 0, 0:16] = residual(vb2, 7, ws2, i2, (16, 32), 2)
+    s3[p + 1, 24:32] = 0.125 * fold_lanes(fold_rows(tmp.at[2, 0], 0), 2)
     y_s3.start()
     k2[7:9, 16:32] = vb2[7:9, 16:32]
     y_k2.start()
@@ -593,8 +585,8 @@
     here, there = va3, vb3
     for at in range(1, BOTTOM):
         halo = BOTTOM + 3 - at
-        planes = (jnp.maximum(1, p + 1 - halo), jnp.minimum(17, p + 2 + halo))
-        sweep(here, there, d3, j3, ws3, planes, rows3 if halo > 8 else (16, 40), 4, BOTTOM_STEPS[at])
+        rows = (12, 44) if halo > 8 else (16, 40)
+        sweep(here, there, d3, j3, ws3, (1, 17), rows, 4, BOTTOM_STEPS[at])
         here, there = there, here
 
     h_k2.arrive()
@@ -607,7 +599,8 @@
                 at = pl.ds(8 + 16 * t + odd, 8, stride=2)
                 va2[a, at] = k2[a, at] + e
 
-    loop(0, 16, finish2)
+    for a in range(16):
+        finish2(a)
     sweep(va2, vb2, d2, j2, ws2, (1, 15), rows2, 2, FINE_STEPS[0])
     sweep(vb2, va2, d2, j2, ws2, (2, 14), rows2, 2, FINE_STEPS[1])
     sweep(va2, vb2, d2, j2, ws2, (3, 13), rows2, 2, FINE_STEPS[2])
@@ -623,7 +616,8 @@
                 at = pl.ds(8 + 16 * t + odd, 8, stride=2)
                 va1[a, at] = k1[a, at] + e
 
-    loop(0, 16, finish1)
+    for a in range(16):
+        finish1(a)
     sweep(va1, vb1, d1, j1, ws1, (1, 15), rows1, 1, FINE_STEPS[0])
     sweep(vb1, va1, d1, j1, ws1, (2, 14), rows1, 1, FINE_STEPS[1])
     sweep(va1, vb1, d1, j1, ws1, (3, 13), rows1, 1, FINE_STEPS[2])
@@ -634,12 +628,14 @@
     def finish0(m):
         for t in range(5):
             e = va1[4 + m, 14 + 8 * t:22 + 8 * t]
-            for x in range(2):
-                a = 1 + 2 * m + x
-                for h in range(2):
+            to_lane = lanes((8, 128)) // 2
+            for h in range(2):
+                half = jnp.take_along_axis(e, to_lane + 64 * h, axis=1)
+                for x in range(2):
+                    a = 1 + 2 * m + x
                     for odd in range(2):
-                        got = pre[a, h, pl.ds(12 + 16 * t + odd, 8, stride=2)]
-                        va[a, h, pl.ds(8 + 16 * t + odd, 8, stride=2)] = got + e
+                        at = pl.ds(12 + 16 * t + odd, 8, stride=2)
+                        va[a, h, at] = pre[a, h, at] + half
 
     loop(0, 8, finish0)
     fine_sweep(va, vb, 0, 3)
@@ -647,14 +643,8 @@
     fine_sweep(va, vb, 2, 1)
     fine_sweep(vb, va, 3, 0)
 
-    def join(x):
-        left, right = shuffle(va[5 + x, 0, 12:76], va[5 + x, 1, 12:76], back)
-        obuf[0, x] = left
-        obuf[1, x] = right
-
-    loop(0, 8, join)
     give = pltpu.make_async_remote_copy(
-        src_ref=obuf.at[1 - k],
+        src_ref=va.at[pl.ds(5, 8), 1 - k, pl.ds(16, 64)],
         dst_ref=out.at[pl.ds(8 * k, 8)],
         send_sem=o_send,
         recv_sem=o_recv,
@@ -662,10 +652,10 @@
         device_id_type=MESH,
     )
     give.start()
-    out[pl.ds(8 * k, 8)] = obuf[k]
+    out[pl.ds(8 * k, 8)] = va[5:13, k, own]
     give.wait_send()
     pltpu.make_async_remote_copy(
-        src_ref=obuf.at[k],
+        src_ref=va.at[pl.ds(5, 8), k, pl.ds(16, 64)],
         dst_ref=out.at[pl.ds(8 * (1 - k), 8)],
         send_sem=o_send,
         recv_sem=o_recv,
@@ -683,10 +673,7 @@
     def buf(*shape):
         return pltpu.VMEM(shape, F32)
 
-    fine = [buf(18, 2, 88, 128)] * 10
-    scratch = [buf(18, 2, 80, 128)] * 3
-    scratch += [pltpu.VMEM((256, 256), jnp.bfloat16)] * 2 + [buf(64, 128)]
-    scratch += fine + [buf(18, 88, 128), buf(18, 2, 88, 128), buf(18, 2, 96, 128), buf(2, 8, 64, 128)]
+    scratch = [buf(18, 2, 96, 128)] * 3 + [buf(4, 2, 64, 128)] + [buf(18, 2, 96, 128)] * 10
     scratch += [buf(16, 64, 128)] * 13
     scratch += [buf(16, 48, 128)] * 13
     scratch += [buf(18, 56, 128)] * 12

time: 104 us -> 82 us (0.79)
  Pallas kernels: 102 us -> 80 us
    pallas_call x1, Pallas kernels: 102 us -> 80 us  [on_device(): pl.pallas_call(kernel, out_shape=jax.ShapeDtypeStruct((16, 64, 128), F32)...]
where the time goes in v2:
time: 82 us; the launch traced here: 81.9 us
  Pallas kernels  80 us (98%)
  local copies, waits for them, and re-layouts  1.89 us (2%)
    pallas_call x1, Pallas kernels, on_device(): pl.pallas_call(kernel, out_shape=jax.ShapeDtypeStruct((16, 64, 128), F32)...  80 us
    unnamed x1, local copies, waits for them, and re-layouts  1.89 us

profile of v2, /device:TPU:7, one launch (start us, length us, event | category | flops | bytes accessed | tf_op | source)
XLA Modules:
  0.0 81.9 jit_solution(14726277641153063191)
XLA Ops:
  0.0 80.0 %vcycle.1 = f32[16,64,128]{2,1,0:T(8,128)} custom-call(f32[16,64,128]{2,1,0:T(8,128)} %iterate.1, f32[16,64,128]{2,1,0:T(8,128)} %right_side.1, f32[16,64,128]{2,1,0:T(8,128)} %diffusion.1), custom_call_target="tpu_custom_call" | custom-call | flops 100000000 | bytes 2000000 | tf_op jit(solution)/shard_map/vcycle/pallas_call | solution.py:684
  80.0 1.9 %copy.5 = f32[16,64,128]{2,1,0:T(8,128)} copy(f32[16,64,128]{2,1,0:T(8,128)} %vcycle.1) | data formatting | bytes 1048576

commit v3 on v2

--- a/solution.py
+++ b/solution.py
@@ -15,6 +15,9 @@
 MESH = pl.DeviceIdType.MESH
 NP = 16
 NJ = 8
+FINE_SEND = 0
+FINE_RECV = 107
+SEMS = 107 + 33 + 8 + 27 + 8 + 4 + 14 + 6 + 4 + 4 + 15 + 2 + 8 + 1
 
 
 def chebyshev_steps(sweeps, low_end, high_end):
@@ -59,8 +62,9 @@
 
 
 class Moves:
-    def __init__(self, place, ref, send, recv, dirs):
-        self.place, self.ref, self.send, self.recv, self.dirs = place, ref, send, recv, dirs
+    def __init__(self, place, ref, sem, send, recv, dirs):
+        self.place, self.ref, self.sem, self.dirs = place, ref, sem, dirs
+        self.send, self.recv = send, recv
 
     def copy(self, at):
         p, j = self.place
@@ -69,8 +73,8 @@
         return pltpu.make_async_remote_copy(
             src_ref=self.ref.at[src],
             dst_ref=self.ref.at[dst],
-            send_sem=self.send.at[at],
-            recv_sem=self.recv.at[at],
+            send_sem=self.sem.at[self.send + at],
+            recv_sem=self.sem.at[self.recv + at],
             device_id=(to // 2, j + dj, to % 2),
             device_id_type=MESH,
         )
@@ -136,14 +140,12 @@
 
 def kernel(
     iterate, right_side, diffusion, out,
-    va, cc, gg, tmp,
-    vb, dd, jj, di, wx, wl, wr, zl, zr, pre,
+    va, cc, gg, tmp, vb, vc, vd, ve,
+    dd, jj, di, wx, wl, wr, zl, zr, pre,
     s1, c1, k1, va1, vb1, d1, j1, i1, wx1, wl1, wr1, zl1, zr1,
-    s2, c2, k2, va2, vb2, d2, j2, i2, wx2, wl2, wr2, zl2, zr2,
-    s3, c3, va3, vb3, d3, j3, i3, wx3, wl3, wr3, zl3, zr3,
-    x_send, x_recv, self_sem,
-    s1_send, s1_recv, s2_send, s2_recv,
-    y_send, y_recv, h_send, h_recv, g_send, g_recv, o_send, o_recv,
+    s2, c2, k2, va2, vb2, d2, j2, i2, wx2, wl2, wr2, zl2, zr2, pc2, pk2,
+    s3, c3, va3, vb3, d3, j3, i3, wx3, wl3, wr3, zl3, zr3, pc3, ps3,
+    sem, self_sem,
 ):
     i = lax.axis_index("gx")
     j = lax.axis_index("gy")
@@ -162,7 +164,7 @@
     count = NP - 1
     for dj in (-1, 1, -2, 2):
         okj = jnp.logical_and(j + dj >= 0, j + dj < NJ)
-        for dp in range(-3, 4) if abs(dj) == 1 else (0,):
+        for dp in range(-2, 3) if abs(dj) == 1 else (0,):
             ok = jnp.logical_and(okj, jnp.logical_and(p + dp >= 0, p + dp < NP))
             count = count + ok.astype(jnp.int32)
 
@@ -174,14 +176,13 @@
 
     def fine_moves(at, src, dst, halo):
         n = 8 + halo
-        sends = []
 
         def copy(slot_s, slot_r, x0, nx, a0, low, size, to, zh, dev):
             return pltpu.make_async_remote_copy(
                 src_ref=src.at[pl.ds(x0, nx), pl.ds(low, size)],
                 dst_ref=dst.at[pl.ds(a0, nx), zh, pl.ds(to, size)],
-                send_sem=x_send.at[at, slot_s],
-                recv_sem=x_recv.at[at, slot_r],
+                send_sem=sem.at[FINE_SEND + 11 * at + slot_s],
+                recv_sem=sem.at[FINE_RECV + 11 * at + slot_r],
                 device_id=dev,
                 device_id_type=MESH,
             )
@@ -192,7 +193,9 @@
             self_sem.at[at],
         )
         other = 1 - k
-        sends.append((None, copy(0, 0, other * (8 - halo), n, 5 - halo * other, 0, 64, 16, k, (i, j, other))))
+        corner = halo - 1
+        ny = 8 + corner
+        sends = []
         rows = [(0, 0, 64, 16), (1, 56, 8, 8), (-1, 0, 8, 80)]
         for dj, low, size, to in rows:
             okj = jnp.logical_and(j + dj >= 0, j + dj < NJ)
@@ -200,13 +203,15 @@
             up = jnp.logical_and(i < 7, okj)
             down = jnp.logical_and(i > 0, okj)
             slot = 1 + 2 * turn + k
-            sends.append((up, copy(1 + 2 * turn, slot, 16 - halo, halo, 5 - halo, low, size, to, k, (i + 1, j + dj, 0))))
-            sends.append((down, copy(2 + 2 * turn, slot, 0, halo, 13, low, size, to, k, (i - 1, j + dj, 1))))
+            w = halo if dj == 0 else corner
+            sends.append((up, copy(1 + 2 * turn, slot, 16 - w, w, 5 - w, low, size, to, k, (i + 1, j + dj, 0))))
+            sends.append((down, copy(2 + 2 * turn, slot, 0, w, 13, low, size, to, k, (i - 1, j + dj, 1))))
             if dj != 0:
                 for half in (0, 1):
                     sends.append(
-                        (okj, copy(5 + 2 * turn + half, 5 + 2 * turn + k, half * (8 - halo), n, 5 - halo * half, low, size, to, k, (i, j + dj, half)))
+                        (okj, copy(5 + 2 * turn + half, 5 + 2 * turn + k, half * (8 - corner), ny, 5 - corner * half, low, size, to, k, (i, j + dj, half)))
                     )
+        sends.append((None, copy(0, 0, other * (8 - halo), n, 5 - halo * other, 0, 64, 16, k, (i, j, other))))
 
         def start():
             mine.start()
@@ -216,19 +221,25 @@
                 else:
                     pl.when(ok)(c.start)
 
-        def arrive():
+        def arrive_inner():
             mine.wait()
             copy(0, 0, 0, n, 5 - halo * k, 0, 64, 16, other, (i, j, other)).wait_recv()
+            for dj, low, size, to in rows[1:]:
+                turn = {1: 1, -1: 2}[dj]
+                okj = jnp.logical_and(j - dj >= 0, j - dj < NJ)
+                for half in (0, 1):
+                    pl.when(okj)(copy(0, 5 + 2 * turn + half, 0, ny, 5 - corner * k, low, size, to, half, (i, j, other)).wait_recv)
+
+        def arrive_outer():
             beside = jnp.logical_or(jnp.logical_and(k == 0, i > 0), jnp.logical_and(k == 1, i < 7))
-            a0 = (5 - halo) * (1 - k) + 13 * k
             for dj, low, size, to in rows:
                 turn = {0: 0, 1: 1, -1: 2}[dj]
                 okj = jnp.logical_and(j - dj >= 0, j - dj < NJ)
                 ok = jnp.logical_and(beside, okj)
+                w = halo if dj == 0 else corner
+                a0 = (5 - w) * (1 - k) + 13 * k
                 for half in (0, 1):
-                    pl.when(ok)(copy(0, 1 + 2 * turn + half, 0, halo, a0, low, size, to, half, (i, j, other)).wait_recv)
-                    if dj != 0:
-                        pl.when(okj)(copy(0, 5 + 2 * turn + half, 0, n, 5 - halo * k, low, size, to, half, (i, j, other)).wait_recv)
+                    pl.when(ok)(copy(0, 1 + 2 * turn + half, 0, w, a0, low, size, to, half, (i, j, other)).wait_recv)
 
         def drain():
             for ok, c in sends:
@@ -237,7 +248,7 @@
                 else:
                     pl.when(ok)(c.wait_send)
 
-        return start, arrive, drain
+        return start, arrive_inner, arrive_outer, drain
 
     moves_c = fine_moves(0, diffusion, cc, 5)
     moves_v = fine_moves(1, iterate, va, 5)
@@ -275,11 +286,13 @@
         clear(ref, 18, low, high, [(j == 0, 8, 8), (j == 7, 80, 8)])
     clear(pre, 18, low, high, [(j == 0, 8, 8), (j == 7, 80, 8)], (5, 13))
     low, high = outer(6, 16, 4, 64)
-    for ref, own in ((s1, None), (c1, (6, 10)), (k1, (6, 10))):
-        clear(ref, 16, low, high, [(j == 0, 8, 8), (j == 7, 48, 8)], own)
+    for ref, owned in ((s1, None), (c1, (6, 10)), (k1, (6, 10))):
+        clear(ref, 16, low, high, [(j == 0, 8, 8), (j == 7, 48, 8)], owned)
     low, high = outer(7, 16, 2, 32)
-    for ref, own in ((s2, None), (c2, (7, 9)), (k2, (7, 9))):
-        clear(ref, 16, low, high, [(j == 0, 8, 8), (j == 7, 32, 8)], own)
+    for ref, owned in ((s2, None), (c2, (7, 9)), (k2, (7, 9))):
+        clear(ref, 16, low, high, [(j == 0, 8, 8), (j == 7, 32, 8)], owned)
+    for ref in (pc2, pk2):
+        clear(ref, 16, low, high, [])
     for ref in (s3, c3):
         clear(ref, 18, 1, 17, [(j == 0, 8, 16), (j == 1, 8, 8), (j == 6, 40, 8), (j == 7, 32, 16)], (p + 1, p + 2))
     for ref in (va3, vb3):
@@ -298,6 +311,25 @@
         low = jnp.take_along_axis(low, from_lane, axis=1)
         high = jnp.take_along_axis(high, from_lane, axis=1)
         return 0.125 * jnp.where(lanes((8, 128)) < 64, low, high)
+
+    def squeeze(ref, a, row, rows, parts):
+        size = rows // parts
+        spot = lanes((size, 128)) % parts
+        res = ref[a, row:row + size]
+        for q in range(1, parts):
+            res = jnp.where(spot == q, ref[a, row + q * size:row + (q + 1) * size], res)
+        return res
+
+    def widen(src, dst, planes, row, rows, parts):
+        size = rows // parts
+        spot = lanes((8, 128))
+        spot = spot - spot % parts
+        for a in planes:
+            for r in range(0, size, 8):
+                value = src[a, r:r + 8]
+                for q in range(parts):
+                    at = row + q * size + r
+                    dst[a, at:at + 8] = jnp.take_along_axis(value, spot + q, axis=1)
 
     own = slice(16, 80)
     moves_c[1]()
@@ -318,31 +350,35 @@
     tmp[2, 0, 0:16] = c2[7, 16:32] + c2[8, 16:32]
     c3[p + 1, 24:32] = 0.125 * fold_lanes(fold_rows(tmp.at[2, 0], 0), 2)
 
-    def y_moves(at, ref, planes, first, row, rows, mid=()):
-        dirs = block_dirs(planes, first, 0, row, rows, (0,), (-1, 1), False, mid)
-        return Moves(place, ref, y_send.at[at], y_recv.at[at], dirs)
-
-    def h_moves(at, ref, planes, first, halo, row, rows, reach, mid=()):
-        dps = [d for d in range(-reach, reach + 1) if d != 0]
-        dirs = block_dirs(planes, first, halo, row, rows, dps, (0,), True, mid)
-        return Moves(place, ref, h_send.at[at], h_recv.at[at], dirs)
-
-    def column_moves(at, ref):
+    used = {"recv": FINE_RECV + 33, "send": 0}
+
+    def moves(ref, send, dirs):
+        recv = used["recv"]
+        used["recv"] = recv + len(dirs)
+        return Moves(place, ref, sem, send, recv, dirs)
+
+    def y_moves(send, ref, planes, first, row, rows, mid=()):
+        return moves(ref, send, block_dirs(planes, first, 0, row, rows, (0,), (-1, 1), False, mid))
+
+    def h_moves(send, ref, planes, first, halo, row, rows, dps, mid=()):
+        return moves(ref, send, block_dirs(planes, first, halo, row, rows, dps, (0,), True, mid))
+
+    def column_moves(send, ref):
         here = (p + 1, pl.ds(24, 8))
-        dirs = [(0, dj, here, (p + 1, pl.ds(24 - 8 * dj, 8))) for dj in (-2, -1, 1, 2)]
-        return Moves(place, ref, y_send.at[at], y_recv.at[at], dirs)
+        return moves(ref, send, [(0, dj, here, (p + 1, pl.ds(24 - 8 * dj, 8))) for dj in (-2, -1, 1, 2)])
 
     class Around:
-        def __init__(self, at, ref):
-            self.at, self.ref = at, ref
+        def __init__(self, send, ref):
+            self.send, self.ref, self.recv = send, ref, used["recv"]
+            used["recv"] += NP - 1
 
         def copy(self, q, plane):
             to = (p + q) % NP
             return pltpu.make_async_remote_copy(
-                src_ref=self.ref.at[plane, pl.ds(8, 40)],
-                dst_ref=self.ref.at[plane, pl.ds(8, 40)],
-                send_sem=g_send.at[self.at, q],
-                recv_sem=g_recv.at[self.at, q],
+                src_ref=self.ref.at[plane],
+                dst_ref=self.ref.at[plane],
+                send_sem=sem.at[self.send + q - 1],
+                recv_sem=sem.at[self.recv + q - 1],
                 device_id=(to // 2, j, to % 2),
                 device_id_type=MESH,
             )
@@ -356,22 +392,26 @@
         def drain(self):
             loop(1, NP, lambda q: self.copy(q, p + 1).wait_send())
 
-    y_c1 = y_moves(0, c1, 4, 6, 16, 32)
-    y_c2 = y_moves(1, c2, 2, 7, 16, 16)
-    y_c3 = column_moves(2, c3)
-    h_c1 = h_moves(0, c1, 4, 6, 6, 16, 32, 2)
-    h_c2 = h_moves(1, c2, 2, 7, 7, 16, 16, 4)
-    h_c3 = Around(0, c3)
-    y_pre = y_moves(3, pre, 8, 5, 16, 64, (slice(None),))
-    h_pre = h_moves(2, pre, 8, 5, 4, 16, 64, 1, (slice(None),))
-    y_k1 = y_moves(4, k1, 4, 6, 16, 32)
-    h_k1 = h_moves(3, k1, 4, 6, 6, 16, 32, 2)
-    y_k2 = y_moves(5, k2, 2, 7, 16, 16)
-    h_k2 = h_moves(4, k2, 2, 7, 7, 16, 16, 4)
-    y_s3 = column_moves(6, s3)
-    h_s3 = Around(1, s3)
-    m_s1 = Moves(place, s1, s1_send, s1_recv, block_dirs(4, 6, 5, 16, 32, range(-2, 3), (0, -1, 1), False))
-    m_s2 = Moves(place, s2, s2_send, s2_recv, block_dirs(2, 7, 6, 16, 16, range(-3, 4), (0, -1, 1), False))
+    y_c1 = y_moves(33, c1, 4, 6, 16, 32)
+    y_c2 = y_moves(35, c2, 2, 7, 16, 16)
+    y_c3 = column_moves(37, c3)
+    h_c1 = h_moves(0, c1, 4, 6, 6, 16, 32, (-2, -1, 1, 2))
+    h_c2 = h_moves(4, pc2, 2, 7, 7, 8, 0, (-4, -3, -2, -1, 1, 2, 3, 4))
+    h_c3 = Around(12, pc3)
+    m_s1 = moves(s1, 41, block_dirs(4, 6, 4, 16, 32, (-1, 0, 1), (0, -1, 1), False))
+    y_pre = y_moves(49, pre, 8, 5, 16, 64, (slice(None),))
+    h_pre = h_moves(51, pre, 8, 5, 4, 16, 64, (-1, 1), (slice(None),))
+    m_s2 = moves(s2, 53, block_dirs(2, 7, 4, 16, 16, (-2, -1, 0, 1, 2), (0, -1, 1), False))
+    y_k1 = y_moves(67, k1, 4, 6, 16, 32)
+    h_k1 = h_moves(69, k1, 4, 6, 6, 16, 32, (-2, -1, 1, 2))
+    h_s1 = h_moves(73, s1, 4, 6, 5, 16, 32, (-2, 2))
+    h_s2 = h_moves(75, s2, 2, 7, 6, 16, 16, (-3, 3))
+    y_s3 = column_moves(77, s3)
+    h_s3 = Around(81, ps3)
+    y_k2 = y_moves(96, k2, 2, 7, 16, 16)
+    h_k2 = h_moves(98, pk2, 2, 7, 7, 8, 0, (-4, -3, -2, -1, 1, 2, 3, 4))
+    out_send, out_recv = 106, used["recv"]
+    assert out_recv < SEMS, out_recv
 
     y_c1.start()
     y_c2.start()
@@ -402,9 +442,11 @@
                 di[a, h, wide] = diag
                 jj[a, h, wide] = jnp.where(mid[h] > 0.0, 1.0 / diag, 0.0)
 
-    wx[0, :, wide] = 0.5 * (cc[0, :, wide] + cc[1, :, wide])
-    spread(1, 16, 2, fine_setup)
-
+    def fine_setups(low, count):
+        wx[low - 1, :, wide] = 0.5 * (cc[low - 1, :, wide] + cc[low, :, wide])
+        spread(low, count, 3, fine_setup)
+
+    fine_setups(6 - 5 * k, 11)
     moves_v[1]()
     moves_g[1]()
 
@@ -428,7 +470,7 @@
                     total = total + zl[a, h, w] * left[h] + zr[a, h, w] * right[h]
                     yield u, a, h, w, mid[h], total
 
-    def fine_sweep(src, dst, step, halo):
+    def fine_sweep(src, dst, step, low_plane, count, most=4):
         keep, new = FINE_STEPS[step]
 
         def run(low, n):
@@ -439,21 +481,24 @@
                 dd[a, h, w] = move
                 dst[a, h, w] = mid + move
 
-        spread(5 - halo, 8 + 2 * halo, 4, run)
-
-    fine_sweep(va, vb, 0, 4)
-    fine_sweep(vb, va, 1, 3)
+        spread(low_plane, count, most, run)
+
+    rounds = ((va, vb), (vb, vc), (vc, vd), (vd, ve))
+    for step, (src, dst) in enumerate(rounds):
+        fine_sweep(src, dst, step, 6 + step - 5 * k, 11 - 2 * step)
+    moves_c[2]()
+    fine_setups(1 + 11 * k, 5)
+    moves_v[2]()
+    moves_g[2]()
+    for moved in (moves_c, moves_v, moves_g):
+        moved[3]()
     y_c1.arrive()
-    y_c2.arrive()
-    y_c3.arrive()
     h_c1.start()
-    h_c2.start()
-    h_c3.start()
-    fine_sweep(va, vb, 2, 2)
-    fine_sweep(vb, va, 3, 1)
+    for step, (src, dst) in enumerate(rounds):
+        fine_sweep(src, dst, step, 1 + step + (11 - 2 * step) * k, 5, 5)
 
     for m in range(4):
-        for u, a, h, w, mid, total in fine_sum(va, 5 + 2 * m, 2, 16, 80):
+        for u, a, h, w, mid, total in fine_sum(ve, 5 + 2 * m, 2, 16, 80):
             part = total - di[a, h, w] * mid
             spot = slice(w.start - 16, w.stop - 16)
             tmp[m, h, spot] = part if u == 0 else tmp[m, h, spot] + part
@@ -463,10 +508,17 @@
     m_s1.start()
 
     def keep_fine(a):
-        pre[a, :, own] = va[a, :, own]
+        pre[a, :, own] = ve[a, :, own]
 
     loop(5, 13, keep_fine)
     y_pre.start()
+    y_c2.arrive()
+    for a in (7, 8):
+        pc2[a] = squeeze(c2, a, 8, 32, 2)
+    h_c2.start()
+    y_c3.arrive()
+    pc3[p + 1] = squeeze(c3, p + 1, 12, 32, 4)
+    h_c3.start()
 
     def setup(c, jn, dn, wxn, wln, wrn, zln, zrn, planes, rows, step, scale):
         low, high = planes
@@ -537,12 +589,9 @@
 
     h_c1.arrive()
     setup(c1, j1, i1, wx1, wl1, wr1, zl1, zr1, (1, 15), rows1, 1, 0.25)
-    h_c2.arrive()
-    setup(c2, j2, i2, wx2, wl2, wr2, zl2, zr2, (1, 15), rows2, 2, 0.0625)
-    h_c3.arrive()
-    setup(c3, j3, i3, wx3, wl3, wr3, zl3, zr3, (1, 17), rows3, 4, 0.015625)
-
     m_s1.arrive()
+    y_pre.arrive()
+    h_pre.start()
     first(va1, d1, s1, j1, (2, 14), rows1, FINE_STEPS[0][1])
     sweep(va1, vb1, d1, j1, ws1, (3, 13), rows1, 1, FINE_STEPS[1])
     sweep(vb1, va1, d1, j1, ws1, (4, 12), rows1, 1, FINE_STEPS[2])
@@ -560,8 +609,11 @@
     m_s2.start()
     k1[6:10, 16:48] = vb1[6:10, 16:48]
     y_k1.start()
-    y_pre.arrive()
-    h_pre.start()
+    h_s1.start()
+    h_c2.arrive()
+    others2 = tuple(range(7)) + tuple(range(9, 16))
+    widen(pc2, c2, others2, 8, 32, 2)
+    setup(c2, j2, i2, wx2, wl2, wr2, zl2, zr2, (1, 15), rows2, 2, 0.0625)
 
     m_s2.arrive()
     first(va2, d2, s2, j2, (3, 13), rows2, FINE_STEPS[0][1])
@@ -576,11 +628,21 @@
     y_k1.arrive()
     h_k1.start()
     y_s3.arrive()
+    ps3[p + 1] = squeeze(s3, p + 1, 12, 32, 4)
     h_s3.start()
     y_k2.arrive()
+    for a in (7, 8):
+        pk2[a] = squeeze(k2, a, 8, 32, 2)
     h_k2.start()
+    h_s2.start()
+    h_c3.arrive()
+    y_c3.drain()
+    widen(pc3, c3, range(1, 17), 12, 32, 4)
+    setup(c3, j3, i3, wx3, wl3, wr3, zl3, zr3, (1, 17), rows3, 4, 0.015625)
 
     h_s3.arrive()
+    y_s3.drain()
+    widen(ps3, s3, range(1, 17), 12, 32, 4)
     first(va3, d3, s3, j3, (1, 17), rows3, BOTTOM_STEPS[0][1])
     here, there = va3, vb3
     for at in range(1, BOTTOM):
@@ -590,6 +652,8 @@
         here, there = there, here
 
     h_k2.arrive()
+    widen(pk2, k2, others2, 8, 32, 2)
+    h_s2.arrive()
 
     def finish2(a):
         up = jnp.clip(p - 3 + (a + 1) // 2, 0, 17)
@@ -607,6 +671,7 @@
     sweep(vb2, va2, d2, j2, ws2, (4, 12), rows2, 2, FINE_STEPS[3])
 
     h_k1.arrive()
+    h_s1.arrive()
 
     def finish1(a):
         up = 4 + a // 2
@@ -638,16 +703,15 @@
                         va[a, h, at] = pre[a, h, at] + half
 
     loop(0, 8, finish0)
-    fine_sweep(va, vb, 0, 3)
-    fine_sweep(vb, va, 1, 2)
-    fine_sweep(va, vb, 2, 1)
-    fine_sweep(vb, va, 3, 0)
-
+    fine_sweep(va, vb, 0, 2, 14)
+    fine_sweep(vb, va, 1, 3, 12)
+    fine_sweep(va, vb, 2, 4, 10)
+    fine_sweep(vb, va, 3, 5, 8)
     give = pltpu.make_async_remote_copy(
         src_ref=va.at[pl.ds(5, 8), 1 - k, pl.ds(16, 64)],
         dst_ref=out.at[pl.ds(8 * k, 8)],
-        send_sem=o_send,
-        recv_sem=o_recv,
+        send_sem=sem.at[out_send],
+        recv_sem=sem.at[out_recv],
         device_id=(i, j, 1 - k),
         device_id_type=MESH,
     )
@@ -657,33 +721,29 @@
     pltpu.make_async_remote_copy(
         src_ref=va.at[pl.ds(5, 8), k, pl.ds(16, 64)],
         dst_ref=out.at[pl.ds(8 * (1 - k), 8)],
-        send_sem=o_send,
-        recv_sem=o_recv,
+        send_sem=sem.at[out_send],
+        recv_sem=sem.at[out_recv],
         device_id=(i, j, 1 - k),
         device_id_type=MESH,
     ).wait_recv()
 
-    for moves in (moves_c, moves_v, moves_g):
-        moves[2]()
-    for moves in (y_c1, y_c2, y_c3, h_c1, h_c2, h_c3, m_s1, y_pre, h_pre, m_s2, y_k1, h_k1, y_s3, h_s3, y_k2, h_k2):
-        moves.drain()
+    for moved in (y_c1, y_c2, h_c1, h_c2, h_c3, m_s1, y_pre, h_pre, m_s2, y_k1, h_k1, h_s1, h_s2, h_s3, y_k2, h_k2):
+        moved.drain()
 
 
 def on_device(iterate, right_side, diffusion):
     def buf(*shape):
         return pltpu.VMEM(shape, F32)
 
-    scratch = [buf(18, 2, 96, 128)] * 3 + [buf(4, 2, 64, 128)] + [buf(18, 2, 96, 128)] * 10
+    scratch = [buf(18, 2, 96, 128)] * 3 + [buf(4, 2, 64, 128)] + [buf(18, 2, 96, 128)] * 13
     scratch += [buf(16, 64, 128)] * 13
-    scratch += [buf(16, 48, 128)] * 13
-    scratch += [buf(18, 56, 128)] * 12
+    scratch += [buf(16, 48, 128)] * 13 + [buf(16, 16, 128)] * 2
+    scratch += [buf(18, 56, 128)] * 12 + [buf(18, 8, 128)] * 2
     dma = pltpu.SemaphoreType.DMA
-    scratch += [dma((3, 11)), dma((3, 11)), dma((3,))]
-    scratch += [dma((14,)), dma((14,)), dma((20,)), dma((20,))]
-    scratch += [dma((7, 4)), dma((7, 4)), dma((5, 8)), dma((5, 8)), dma((2, NP)), dma((2, NP)), dma, dma]
+    scratch += [dma((SEMS,)), dma((3,))]
     return pl.pallas_call(
         kernel,
-        out_shape=jax.ShapeDtypeStruct((16, 64, 128), F32),
+        out_shape=pltpu.VMEM((16, 64, 128), F32),
         in_specs=[pl.BlockSpec(memory_space=pl.ANY)] * 3,
         out_specs=pl.BlockSpec(memory_space=pltpu.VMEM),
         scratch_shapes=scratch,

time: 82 us -> 72.6 us (0.89)
  the two profiles are of different devices: /device:TPU:7 before, /device:TPU:5 now
where the time goes in v3:
time: 72.6 us; the launch traced here: 72.5 us
  Pallas kernels  71.7 us (99%)
  local copies, waits for them, and re-layouts  0.8 us (1%)
    pallas_call x1, Pallas kernels, on_device(): pl.pallas_call(kernel, out_shape=pltpu.VMEM((16, 64, 128), F32), in_specs...  71.7 us

profile of v3, /device:TPU:5, one launch (start us, length us, event | category | flops | bytes accessed | tf_op | source)
XLA Modules:
  0.0 72.5 jit_solution(6096975493620263027)
XLA Ops:
  0.0 71.7 %vcycle.1 = f32[16,64,128]{2,1,0:T(8,128)S(1)} custom-call(f32[16,64,128]{2,1,0:T(8,128)} %iterate.1, f32[16,64,128]{2,1,0:T(8,128)} %right_side.1, f32[16,64,128]{2,1,0:T(8,128)} %diffusion.1), custom_call_target="tpu_custom_call" | custom-call | flops 100000000 | bytes 2000000 | tf_op jit(solution)/shard_map/vcycle/pallas_call | solution.py:744
  71.7 0.8 %copy.5 = f32[16,64,128]{2,1,0:T(8,128)} copy(f32[16,64,128]{2,1,0:T(8,128)S(1)} %vcycle.1) | data formatting | bytes 1048576

commit v4 on v3

--- a/solution.py
+++ b/solution.py
@@ -16,8 +16,8 @@
 NP = 16
 NJ = 8
 FINE_SEND = 0
-FINE_RECV = 107
-SEMS = 107 + 33 + 8 + 27 + 8 + 4 + 14 + 6 + 4 + 4 + 15 + 2 + 8 + 1
+FINE_RECV = 111
+SEMS = 111 + 33 + 6 + 27 + 8 + 4 + 24 + 6 + 4 + 15 + 2 + 8 + 1
 
 
 def chebyshev_steps(sweeps, low_end, high_end):
@@ -164,7 +164,7 @@
     count = NP - 1
     for dj in (-1, 1, -2, 2):
         okj = jnp.logical_and(j + dj >= 0, j + dj < NJ)
-        for dp in range(-2, 3) if abs(dj) == 1 else (0,):
+        for dp in range(-2, 3):
             ok = jnp.logical_and(okj, jnp.logical_and(p + dp >= 0, p + dp < NP))
             count = count + ok.astype(jnp.int32)
 
@@ -195,6 +195,7 @@
         other = 1 - k
         corner = halo - 1
         ny = 8 + corner
+        inner = [(None, copy(0, 0, other * (8 - halo), n, 5 - halo * other, 0, 64, 16, k, (i, j, other)))]
         sends = []
         rows = [(0, 0, 64, 16), (1, 56, 8, 8), (-1, 0, 8, 80)]
         for dj, low, size, to in rows:
@@ -208,14 +209,14 @@
             sends.append((down, copy(2 + 2 * turn, slot, 0, w, 13, low, size, to, k, (i - 1, j + dj, 1))))
             if dj != 0:
                 for half in (0, 1):
-                    sends.append(
+                    inner.append(
                         (okj, copy(5 + 2 * turn + half, 5 + 2 * turn + k, half * (8 - corner), ny, 5 - corner * half, low, size, to, k, (i, j + dj, half)))
                     )
-        sends.append((None, copy(0, 0, other * (8 - halo), n, 5 - halo * other, 0, 64, 16, k, (i, j, other))))
-
-        def start():
-            mine.start()
-            for ok, c in sends:
+
+        def start(part):
+            if part == 0:
+                mine.start()
+            for ok, c in (inner, sends)[part]:
                 if ok is None:
                     c.start()
                 else:
@@ -242,7 +243,7 @@
                     pl.when(ok)(copy(0, 1 + 2 * turn + half, 0, w, a0, low, size, to, half, (i, j, other)).wait_recv)
 
         def drain():
-            for ok, c in sends:
+            for ok, c in inner + sends:
                 if ok is None:
                     c.wait_send()
                 else:
@@ -253,9 +254,9 @@
     moves_c = fine_moves(0, diffusion, cc, 5)
     moves_v = fine_moves(1, iterate, va, 5)
     moves_g = fine_moves(2, right_side, gg, 4)
-    moves_c[0]()
-    moves_v[0]()
-    moves_g[0]()
+    for part in range(2):
+        for moved in (moves_c, moves_v, moves_g):
+            moved[0](part)
 
     def clear(ref, planes, low_planes, high_from, edges, own=None):
         def wipe(a):
@@ -289,13 +290,12 @@
     for ref, owned in ((s1, None), (c1, (6, 10)), (k1, (6, 10))):
         clear(ref, 16, low, high, [(j == 0, 8, 8), (j == 7, 48, 8)], owned)
     low, high = outer(7, 16, 2, 32)
-    for ref, owned in ((s2, None), (c2, (7, 9)), (k2, (7, 9))):
-        clear(ref, 16, low, high, [(j == 0, 8, 8), (j == 7, 32, 8)], owned)
+    for ref, owned in ((s2, None), (c2, (7, 9))):
+        clear(ref, 16, low, high, [(j == 0, 8, 32), (j == 1, 8, 16), (j == 6, 72, 16), (j == 7, 56, 32)], owned)
+    clear(k2, 16, low, high, [(j == 0, 32, 8), (j == 7, 56, 8)], (7, 9))
     for ref in (pc2, pk2):
         clear(ref, 16, low, high, [])
-    for ref in (s3, c3):
-        clear(ref, 18, 1, 17, [(j == 0, 8, 16), (j == 1, 8, 8), (j == 6, 40, 8), (j == 7, 32, 16)], (p + 1, p + 2))
-    for ref in (va3, vb3):
+    for ref in (c3, va3, vb3):
         clear(ref, 18, 1, 17, [])
 
     def fold_rows(ref, at):
@@ -346,9 +346,7 @@
     for m in range(2):
         tmp[m, 0, 0:32] = c1[6 + 2 * m, 16:48] + c1[7 + 2 * m, 16:48]
         for t in range(2):
-            c2[7 + m, 16 + 8 * t:24 + 8 * t] = 0.125 * fold_lanes(fold_rows(tmp.at[m, 0], t), 1)
-    tmp[2, 0, 0:16] = c2[7, 16:32] + c2[8, 16:32]
-    c3[p + 1, 24:32] = 0.125 * fold_lanes(fold_rows(tmp.at[2, 0], 0), 2)
+            c2[7 + m, 40 + 8 * t:48 + 8 * t] = 0.125 * fold_lanes(fold_rows(tmp.at[m, 0], t), 1)
 
     used = {"recv": FINE_RECV + 33, "send": 0}
 
@@ -363,9 +361,15 @@
     def h_moves(send, ref, planes, first, halo, row, rows, dps, mid=()):
         return moves(ref, send, block_dirs(planes, first, halo, row, rows, dps, (0,), True, mid))
 
-    def column_moves(send, ref):
-        here = (p + 1, pl.ds(24, 8))
-        return moves(ref, send, [(0, dj, here, (p + 1, pl.ds(24 - 8 * dj, 8))) for dj in (-2, -1, 1, 2)])
+    def column_moves(send, ref, dps, djs):
+        dirs = []
+        for dp, dj, src, dst in block_dirs(2, 7, 4, 40, 16, dps, (0,), False):
+            dirs.append((dp, 0, src, dst))
+        for dj in djs:
+            for dp in (0,) + tuple(dps):
+                row = pl.ds(40 - 16 * dj, 16)
+                dirs.append((dp, dj, (pl.ds(7, 2), pl.ds(40, 16)), (pl.ds(7 - 2 * dp, 2), row)))
+        return moves(ref, send, dirs)
 
     class Around:
         def __init__(self, send, ref):
@@ -393,29 +397,26 @@
             loop(1, NP, lambda q: self.copy(q, p + 1).wait_send())
 
     y_c1 = y_moves(33, c1, 4, 6, 16, 32)
-    y_c2 = y_moves(35, c2, 2, 7, 16, 16)
-    y_c3 = column_moves(37, c3)
+    y_c2 = column_moves(35, c2, (), (-2, -1, 1, 2))
     h_c1 = h_moves(0, c1, 4, 6, 6, 16, 32, (-2, -1, 1, 2))
-    h_c2 = h_moves(4, pc2, 2, 7, 7, 8, 0, (-4, -3, -2, -1, 1, 2, 3, 4))
+    h_c2 = h_moves(4, pc2, 2, 7, 7, 8, 24, (-4, -3, -2, -1, 1, 2, 3, 4))
     h_c3 = Around(12, pc3)
-    m_s1 = moves(s1, 41, block_dirs(4, 6, 4, 16, 32, (-1, 0, 1), (0, -1, 1), False))
-    y_pre = y_moves(49, pre, 8, 5, 16, 64, (slice(None),))
-    h_pre = h_moves(51, pre, 8, 5, 4, 16, 64, (-1, 1), (slice(None),))
-    m_s2 = moves(s2, 53, block_dirs(2, 7, 4, 16, 16, (-2, -1, 0, 1, 2), (0, -1, 1), False))
-    y_k1 = y_moves(67, k1, 4, 6, 16, 32)
-    h_k1 = h_moves(69, k1, 4, 6, 6, 16, 32, (-2, -1, 1, 2))
-    h_s1 = h_moves(73, s1, 4, 6, 5, 16, 32, (-2, 2))
-    h_s2 = h_moves(75, s2, 2, 7, 6, 16, 16, (-3, 3))
-    y_s3 = column_moves(77, s3)
-    h_s3 = Around(81, ps3)
-    y_k2 = y_moves(96, k2, 2, 7, 16, 16)
-    h_k2 = h_moves(98, pk2, 2, 7, 7, 8, 0, (-4, -3, -2, -1, 1, 2, 3, 4))
-    out_send, out_recv = 106, used["recv"]
+    m_s1 = moves(s1, 39, block_dirs(4, 6, 4, 16, 32, (-1, 0, 1), (0, -1, 1), False))
+    y_pre = y_moves(47, pre, 8, 5, 16, 64, (slice(None),))
+    h_pre = h_moves(49, pre, 8, 5, 4, 16, 64, (-1, 1), (slice(None),))
+    m_s2 = column_moves(51, s2, (-2, -1, 1, 2), (-2, -1, 1, 2))
+    y_k1 = y_moves(75, k1, 4, 6, 16, 32)
+    h_k1 = h_moves(77, k1, 4, 6, 6, 16, 32, (-2, -1, 1, 2))
+    h_s1 = h_moves(81, s1, 4, 6, 5, 16, 32, (-2, 2))
+    h_s2 = h_moves(83, s2, 2, 7, 6, 40, 16, (-3, 3))
+    h_s3 = Around(85, ps3)
+    y_k2 = y_moves(100, k2, 2, 7, 40, 16)
+    h_k2 = h_moves(102, pk2, 2, 7, 7, 8, 0, (-4, -3, -2, -1, 1, 2, 3, 4))
+    out_send, out_recv = 110, used["recv"]
     assert out_recv < SEMS, out_recv
 
     y_c1.start()
     y_c2.start()
-    y_c3.start()
 
     wide = slice(12, 84)
     lane = lanes((72, 128))
@@ -514,9 +515,11 @@
     y_pre.start()
     y_c2.arrive()
     for a in (7, 8):
-        pc2[a] = squeeze(c2, a, 8, 32, 2)
+        pc2[a] = squeeze(c2, a, 8, 80, 2)
     h_c2.start()
-    y_c3.arrive()
+    tmp[2, 0] = c2[7, 16:80] + c2[8, 16:80]
+    for t in range(4):
+        c3[p + 1, 12 + 8 * t:20 + 8 * t] = 0.125 * fold_lanes(fold_rows(tmp.at[2, 0], t), 2)
     pc3[p + 1] = squeeze(c3, p + 1, 12, 32, 4)
     h_c3.start()
 
@@ -585,13 +588,11 @@
     ws1 = (s1, wx1, wl1, wr1, zl1, zr1)
     ws2 = (s2, wx2, wl2, wr2, zl2, zr2)
     ws3 = (s3, wx3, wl3, wr3, zl3, zr3)
-    rows1, rows2, rows3 = (8, 56), (8, 40), (8, 48)
+    rows1, wide2, rows2, rows3 = (8, 56), (8, 88), (32, 64), (8, 48)
 
     h_c1.arrive()
     setup(c1, j1, i1, wx1, wl1, wr1, zl1, zr1, (1, 15), rows1, 1, 0.25)
     m_s1.arrive()
-    y_pre.arrive()
-    h_pre.start()
     first(va1, d1, s1, j1, (2, 14), rows1, FINE_STEPS[0][1])
     sweep(va1, vb1, d1, j1, ws1, (3, 13), rows1, 1, FINE_STEPS[1])
     sweep(vb1, va1, d1, j1, ws1, (4, 12), rows1, 1, FINE_STEPS[2])
@@ -605,43 +606,46 @@
         tmp[m, 0, 0:32] = residual(vb1, 6 + 2 * m, ws1, i1, (16, 48), 1)
     for m in range(2):
         for t in range(2):
-            s2[7 + m, 16 + 8 * t:24 + 8 * t] = 0.125 * fold_lanes(fold_rows(tmp.at[m, 0], t), 1)
+            s2[7 + m, 40 + 8 * t:48 + 8 * t] = 0.125 * fold_lanes(fold_rows(tmp.at[m, 0], t), 1)
     m_s2.start()
     k1[6:10, 16:48] = vb1[6:10, 16:48]
     y_k1.start()
     h_s1.start()
+    y_pre.arrive()
+    h_pre.start()
     h_c2.arrive()
     others2 = tuple(range(7)) + tuple(range(9, 16))
-    widen(pc2, c2, others2, 8, 32, 2)
-    setup(c2, j2, i2, wx2, wl2, wr2, zl2, zr2, (1, 15), rows2, 2, 0.0625)
+    widen(pc2, c2, others2, 8, 80, 2)
+    setup(c2, j2, i2, wx2, wl2, wr2, zl2, zr2, (1, 15), wide2, 2, 0.0625)
+    for moved in (y_c1, y_c2, h_c1, h_c2, m_s1, y_pre):
+        moved.drain()
 
     m_s2.arrive()
-    first(va2, d2, s2, j2, (3, 13), rows2, FINE_STEPS[0][1])
-    sweep(va2, vb2, d2, j2, ws2, (4, 12), rows2, 2, FINE_STEPS[1])
-    sweep(vb2, va2, d2, j2, ws2, (5, 11), rows2, 2, FINE_STEPS[2])
-    sweep(va2, vb2, d2, j2, ws2, (6, 10), rows2, 2, FINE_STEPS[3])
-    tmp[2, 0, 0:16] = residual(vb2, 7, ws2, i2, (16, 32), 2)
-    s3[p + 1, 24:32] = 0.125 * fold_lanes(fold_rows(tmp.at[2, 0], 0), 2)
-    y_s3.start()
-    k2[7:9, 16:32] = vb2[7:9, 16:32]
+    first(va2, d2, s2, j2, (3, 13), wide2, FINE_STEPS[0][1])
+    sweep(va2, vb2, d2, j2, ws2, (4, 12), wide2, 2, FINE_STEPS[1])
+    sweep(vb2, va2, d2, j2, ws2, (5, 11), wide2, 2, FINE_STEPS[2])
+    sweep(va2, vb2, d2, j2, ws2, (6, 10), wide2, 2, FINE_STEPS[3])
+    tmp[2, 0] = residual(vb2, 7, ws2, i2, (16, 80), 2)
+    for t in range(4):
+        s3[p + 1, 12 + 8 * t:20 + 8 * t] = 0.125 * fold_lanes(fold_rows(tmp.at[2, 0], t), 2)
+    ps3[p + 1] = squeeze(s3, p + 1, 12, 32, 4)
+    h_s3.start()
+    k2[7:9, 40:56] = vb2[7:9, 40:56]
     y_k2.start()
     y_k1.arrive()
     h_k1.start()
-    y_s3.arrive()
-    ps3[p + 1] = squeeze(s3, p + 1, 12, 32, 4)
-    h_s3.start()
+    h_s2.start()
+    h_c3.arrive()
+    widen(pc3, c3, range(1, 17), 12, 32, 4)
+    setup(c3, j3, i3, wx3, wl3, wr3, zl3, zr3, (1, 17), rows3, 4, 0.015625)
     y_k2.arrive()
     for a in (7, 8):
-        pk2[a] = squeeze(k2, a, 8, 32, 2)
+        pk2[a] = squeeze(k2, a, 32, 32, 2)
     h_k2.start()
-    h_s2.start()
-    h_c3.arrive()
-    y_c3.drain()
-    widen(pc3, c3, range(1, 17), 12, 32, 4)
-    setup(c3, j3, i3, wx3, wl3, wr3, zl3, zr3, (1, 17), rows3, 4, 0.015625)
+    for moved in (h_c3, h_pre, m_s2, y_k1, h_s1, y_k2):
+        moved.drain()
 
     h_s3.arrive()
-    y_s3.drain()
     widen(ps3, s3, range(1, 17), 12, 32, 4)
     first(va3, d3, s3, j3, (1, 17), rows3, BOTTOM_STEPS[0][1])
     here, there = va3, vb3
@@ -652,7 +656,7 @@
         here, there = there, here
 
     h_k2.arrive()
-    widen(pk2, k2, others2, 8, 32, 2)
+    widen(pk2, k2, others2, 32, 32, 2)
     h_s2.arrive()
 
     def finish2(a):
@@ -660,7 +664,7 @@
         for t in range(2):
             e = here[up, 20 + 8 * t:28 + 8 * t]
             for odd in range(2):
-                at = pl.ds(8 + 16 * t + odd, 8, stride=2)
+                at = pl.ds(32 + 16 * t + odd, 8, stride=2)
                 va2[a, at] = k2[a, at] + e
 
     for a in range(16):
@@ -676,7 +680,7 @@
     def finish1(a):
         up = 4 + a // 2
         for t in range(3):
-            e = va2[up, 12 + 8 * t:20 + 8 * t]
+            e = va2[up, 36 + 8 * t:44 + 8 * t]
             for odd in range(2):
                 at = pl.ds(8 + 16 * t + odd, 8, stride=2)
                 va1[a, at] = k1[a, at] + e
@@ -689,6 +693,8 @@
     sweep(vb1, va1, d1, j1, ws1, (4, 12), rows1, 1, FINE_STEPS[3])
 
     h_pre.arrive()
+    for moved in (h_k1, h_s2, h_s3, h_k2):
+        moved.drain()
 
     def finish0(m):
         for t in range(5):
@@ -727,9 +733,6 @@
         device_id_type=MESH,
     ).wait_recv()
 
-    for moved in (y_c1, y_c2, h_c1, h_c2, h_c3, m_s1, y_pre, h_pre, m_s2, y_k1, h_k1, h_s1, h_s2, h_s3, y_k2, h_k2):
-        moved.drain()
-
 
 def on_device(iterate, right_side, diffusion):
     def buf(*shape):
@@ -737,7 +740,7 @@
 
     scratch = [buf(18, 2, 96, 128)] * 3 + [buf(4, 2, 64, 128)] + [buf(18, 2, 96, 128)] * 13
     scratch += [buf(16, 64, 128)] * 13
-    scratch += [buf(16, 48, 128)] * 13 + [buf(16, 16, 128)] * 2
+    scratch += [buf(16, 96, 128)] * 13 + [buf(16, 40, 128), buf(16, 16, 128)]
     scratch += [buf(18, 56, 128)] * 12 + [buf(18, 8, 128)] * 2
     dma = pltpu.SemaphoreType.DMA
     scratch += [dma((SEMS,)), dma((3,))]

time: 72.6 us -> 67.6 us (0.931); the launches traced: 72.5 us -> 66.5 us
  Pallas kernels: 71.7 us -> 65.7 us
    pallas_call x1, Pallas kernels: 71.7 us -> 65.7 us  [on_device(): pl.pallas_call(kernel, out_shape=pltpu.VMEM((16, 64, 128), F32), in_specs...]
where the time goes in v4:
time: 67.6 us; the launch traced here: 66.5 us
  Pallas kernels  65.7 us (97%)
  local copies, waits for them, and re-layouts  0.8 us (1%)
    pallas_call x1, Pallas kernels, on_device(): pl.pallas_call(kernel, out_shape=pltpu.VMEM((16, 64, 128), F32), in_specs...  65.7 us

profile of v4, /device:TPU:5, one launch (start us, length us, event | category | flops | bytes accessed | tf_op | source)
XLA Modules:
  0.0 66.5 jit_solution(9664114294413524149)
XLA Ops:
  0.0 65.7 %vcycle.1 = f32[16,64,128]{2,1,0:T(8,128)S(1)} custom-call(f32[16,64,128]{2,1,0:T(8,128)} %iterate.1, f32[16,64,128]{2,1,0:T(8,128)} %right_side.1, f32[16,64,128]{2,1,0:T(8,128)} %diffusion.1), custom_call_target="tpu_custom_call" | custom-call | flops 100000000 | bytes 2000000 | tf_op jit(solution)/shard_map/vcycle/pallas_call | solution.py:747
  65.7 0.8 %copy.5 = f32[16,64,128]{2,1,0:T(8,128)} copy(f32[16,64,128]{2,1,0:T(8,128)S(1)} %vcycle.1) | data formatting | bytes 1048576

commit v5 on v4

--- a/solution.py
+++ b/solution.py
@@ -16,8 +16,8 @@
 NP = 16
 NJ = 8
 FINE_SEND = 0
-FINE_RECV = 111
-SEMS = 111 + 33 + 6 + 27 + 8 + 4 + 24 + 6 + 4 + 15 + 2 + 8 + 1
+FINE_RECV = 95
+SEMS = 95 + 33 + 6 + 13 + 8 + 4 + 24 + 6 + 4 + 1 + 8 + 1
 
 
 def chebyshev_steps(sweeps, low_end, high_end):
@@ -292,7 +292,6 @@
     low, high = outer(7, 16, 2, 32)
     for ref, owned in ((s2, None), (c2, (7, 9))):
         clear(ref, 16, low, high, [(j == 0, 8, 32), (j == 1, 8, 16), (j == 6, 72, 16), (j == 7, 56, 32)], owned)
-    clear(k2, 16, low, high, [(j == 0, 32, 8), (j == 7, 56, 8)], (7, 9))
     for ref in (pc2, pk2):
         clear(ref, 16, low, high, [])
     for ref in (c3, va3, vb3):
@@ -374,27 +373,31 @@
     class Around:
         def __init__(self, send, ref):
             self.send, self.ref, self.recv = send, ref, used["recv"]
-            used["recv"] += NP - 1
-
-        def copy(self, q, plane):
+            used["recv"] += 1
+
+        def copy(self, q, src, dst):
             to = (p + q) % NP
             return pltpu.make_async_remote_copy(
-                src_ref=self.ref.at[plane],
-                dst_ref=self.ref.at[plane],
-                send_sem=sem.at[self.send + q - 1],
-                recv_sem=sem.at[self.recv + q - 1],
+                src_ref=self.ref.at[src],
+                dst_ref=self.ref.at[dst],
+                send_sem=sem.at[self.send],
+                recv_sem=sem.at[self.recv],
                 device_id=(to // 2, j, to % 2),
                 device_id_type=MESH,
             )
 
         def start(self):
-            loop(1, NP, lambda q: self.copy(q, p + 1).start())
+            loop(1, NP, lambda q: self.copy(q, p + 1, p + 1).start())
+
+        def all(self):
+            planes = pl.ds(1, NP - 1)
+            return self.copy(1, planes, planes)
 
         def arrive(self):
-            loop(1, NP, lambda q: self.copy(q, (p - q + NP) % NP + 1).wait_recv())
+            self.all().wait_recv()
 
         def drain(self):
-            loop(1, NP, lambda q: self.copy(q, p + 1).wait_send())
+            self.all().wait_send()
 
     y_c1 = y_moves(33, c1, 4, 6, 16, 32)
     y_c2 = column_moves(35, c2, (), (-2, -1, 1, 2))
@@ -410,9 +413,8 @@
     h_s1 = h_moves(81, s1, 4, 6, 5, 16, 32, (-2, 2))
     h_s2 = h_moves(83, s2, 2, 7, 6, 40, 16, (-3, 3))
     h_s3 = Around(85, ps3)
-    y_k2 = y_moves(100, k2, 2, 7, 40, 16)
-    h_k2 = h_moves(102, pk2, 2, 7, 7, 8, 0, (-4, -3, -2, -1, 1, 2, 3, 4))
-    out_send, out_recv = 110, used["recv"]
+    h_k2 = h_moves(86, pk2, 2, 7, 7, 8, 0, (-4, -3, -2, -1, 1, 2, 3, 4))
+    out_send, out_recv = 94, used["recv"]
     assert out_recv < SEMS, out_recv
 
     y_c1.start()
@@ -630,19 +632,17 @@
         s3[p + 1, 12 + 8 * t:20 + 8 * t] = 0.125 * fold_lanes(fold_rows(tmp.at[2, 0], t), 2)
     ps3[p + 1] = squeeze(s3, p + 1, 12, 32, 4)
     h_s3.start()
-    k2[7:9, 40:56] = vb2[7:9, 40:56]
-    y_k2.start()
+    k2[7:9, 32:64] = vb2[7:9, 32:64]
+    for a in (7, 8):
+        pk2[a] = squeeze(vb2, a, 32, 32, 2)
+    h_k2.start()
     y_k1.arrive()
     h_k1.start()
     h_s2.start()
     h_c3.arrive()
     widen(pc3, c3, range(1, 17), 12, 32, 4)
     setup(c3, j3, i3, wx3, wl3, wr3, zl3, zr3, (1, 17), rows3, 4, 0.015625)
-    y_k2.arrive()
-    for a in (7, 8):
-        pk2[a] = squeeze(k2, a, 32, 32, 2)
-    h_k2.start()
-    for moved in (h_c3, h_pre, m_s2, y_k1, h_s1, y_k2):
+    for moved in (h_c3, h_pre, m_s2, y_k1, h_s1):
         moved.drain()
 
     h_s3.arrive()

time: 67.6 us -> 65.7 us (0.972); the launches traced: 66.5 us -> 65.6 us
  Pallas kernels: 65.7 us -> 64.8 us
    pallas_call x1, Pallas kernels: 65.7 us -> 64.8 us  [on_device(): pl.pallas_call(kernel, out_shape=pltpu.VMEM((16, 64, 128), F32), in_specs...]
where the time goes in v5:
time: 65.7 us; the launch traced here: 65.6 us
  Pallas kernels  64.8 us (99%)
  local copies, waits for them, and re-layouts  0.8 us (1%)
    pallas_call x1, Pallas kernels, on_device(): pl.pallas_call(kernel, out_shape=pltpu.VMEM((16, 64, 128), F32), in_specs...  64.8 us

profile of v5, /device:TPU:5, one launch (start us, length us, event | category | flops | bytes accessed | tf_op | source)
XLA Modules:
  0.0 65.6 jit_solution(2592458791805965238)
XLA Ops:
  0.0 64.8 %vcycle.1 = f32[16,64,128]{2,1,0:T(8,128)S(1)} custom-call(f32[16,64,128]{2,1,0:T(8,128)} %iterate.1, f32[16,64,128]{2,1,0:T(8,128)} %right_side.1, f32[16,64,128]{2,1,0:T(8,128)} %diffusion.1), custom_call_target="tpu_custom_call" | custom-call | flops 100000000 | bytes 2000000 | tf_op jit(solution)/shard_map/vcycle/pallas_call | solution.py:747
  64.8 0.8 %copy.5 = f32[16,64,128]{2,1,0:T(8,128)} copy(f32[16,64,128]{2,1,0:T(8,128)S(1)} %vcycle.1) | data formatting | bytes 1048576

commit v6 on v5

--- a/solution.py
+++ b/solution.py
@@ -145,6 +145,7 @@
     s1, c1, k1, va1, vb1, d1, j1, i1, wx1, wl1, wr1, zl1, zr1,
     s2, c2, k2, va2, vb2, d2, j2, i2, wx2, wl2, wr2, zl2, zr2, pc2, pk2,
     s3, c3, va3, vb3, d3, j3, i3, wx3, wl3, wr3, zl3, zr3, pc3, ps3,
+    face, yb, yd, ry, rd,
     sem, self_sem,
 ):
     i = lax.axis_index("gx")
@@ -153,6 +154,13 @@
     p = 2 * i + k
     place = (p, j)
 
+    faces = []
+    for at, src in enumerate((diffusion, iterate, right_side)):
+        for t, low in enumerate((56, 0)):
+            faces.append(pltpu.make_async_copy(src.at[pl.ds(0, 16), pl.ds(low, 8)], face.at[at, t], self_sem.at[3 + 2 * at + t]))
+    for load in faces:
+        load.start()
+
     barrier = pltpu.get_barrier_semaphore()
 
     def greet(to, tj):
@@ -172,6 +180,19 @@
             def _():
                 greet(p + dp, j + dj)
 
+    for load in faces:
+        load.wait()
+
+    def pack_faces(at):
+        for t, low in enumerate((3, 0)):
+            for m in range(12):
+                for half in range(2):
+                    yb[at, t, half, 5 * m:5 * m + 5] = face[at, t, m + 4 * half, low:low + 5]
+            for m in range(4):
+                for end in range(2):
+                    yd[at, t, end, 5 * m:5 * m + 5] = face[at, t, m + 12 * (1 - end), low:low + 5]
+
+    loop(0, 3, pack_faces)
     pl.semaphore_wait(barrier, count)
 
     def fine_moves(at, src, dst, halo):
@@ -193,25 +214,31 @@
             self_sem.at[at],
         )
         other = 1 - k
-        corner = halo - 1
-        ny = 8 + corner
+        def outer_rows(slot_s, slot_r, src_rows, dst_rows, dev):
+            return pltpu.make_async_remote_copy(
+                src_ref=src_rows,
+                dst_ref=dst_rows,
+                send_sem=sem.at[FINE_SEND + 11 * at + slot_s],
+                recv_sem=sem.at[FINE_RECV + 11 * at + slot_r],
+                device_id=dev,
+                device_id_type=MESH,
+            )
+
         inner = [(None, copy(0, 0, other * (8 - halo), n, 5 - halo * other, 0, 64, 16, k, (i, j, other)))]
         sends = []
-        rows = [(0, 0, 64, 16), (1, 56, 8, 8), (-1, 0, 8, 80)]
-        for dj, low, size, to in rows:
+        sends.append((i < 7, copy(1, 1 + k, 16 - halo, halo, 5 - halo, 0, 64, 16, k, (i + 1, j, 0))))
+        sends.append((i > 0, copy(2, 1 + k, 0, halo, 13, 0, 64, 16, k, (i - 1, j, 1))))
+        turns = ((0, 1, 11), (1, -1, 80))
+        for t, dj, to in turns:
             okj = jnp.logical_and(j + dj >= 0, j + dj < NJ)
-            turn = {0: 0, 1: 1, -1: 2}[dj]
             up = jnp.logical_and(i < 7, okj)
             down = jnp.logical_and(i > 0, okj)
-            slot = 1 + 2 * turn + k
-            w = halo if dj == 0 else corner
-            sends.append((up, copy(1 + 2 * turn, slot, 16 - w, w, 5 - w, low, size, to, k, (i + 1, j + dj, 0))))
-            sends.append((down, copy(2 + 2 * turn, slot, 0, w, 13, low, size, to, k, (i - 1, j + dj, 1))))
-            if dj != 0:
-                for half in (0, 1):
-                    inner.append(
-                        (okj, copy(5 + 2 * turn + half, 5 + 2 * turn + k, half * (8 - corner), ny, 5 - corner * half, low, size, to, k, (i, j + dj, half)))
-                    )
+            slot = 3 + 2 * t
+            sends.append((up, outer_rows(slot, slot + k, yd.at[at, t, 0], rd.at[at, t, k], (i + 1, j + dj, 0))))
+            sends.append((down, outer_rows(slot + 1, slot + k, yd.at[at, t, 1], rd.at[at, t, k], (i - 1, j + dj, 1))))
+            slot = 7 + 2 * t
+            for half in (0, 1):
+                inner.append((okj, outer_rows(slot + half, slot + k, yb.at[at, t, half], ry.at[at, t, k], (i, j + dj, half))))
 
         def start(part):
             if part == 0:
@@ -222,25 +249,38 @@
                 else:
                     pl.when(ok)(c.start)
 
+        def unpack(buf, t, to, first, planes):
+            for half in (0, 1):
+                for m in range(planes):
+                    dst[first + m, half, to:to + 5] = buf[at, t, half, 5 * m:5 * m + 5]
+
         def arrive_inner():
             mine.wait()
             copy(0, 0, 0, n, 5 - halo * k, 0, 64, 16, other, (i, j, other)).wait_recv()
-            for dj, low, size, to in rows[1:]:
-                turn = {1: 1, -1: 2}[dj]
-                okj = jnp.logical_and(j - dj >= 0, j - dj < NJ)
-                for half in (0, 1):
-                    pl.when(okj)(copy(0, 5 + 2 * turn + half, 0, ny, 5 - corner * k, low, size, to, half, (i, j, other)).wait_recv)
+            for t, dj, to in turns:
+
+                @pl.when(jnp.logical_and(j - dj >= 0, j - dj < NJ))
+                def _():
+                    for half in (0, 1):
+                        outer_rows(0, 7 + 2 * t + half, yb.at[at, t, 0], ry.at[at, t, half], (i, j, other)).wait_recv()
+                    unpack(ry, t, to, 5 - 4 * k, 12)
 
         def arrive_outer():
             beside = jnp.logical_or(jnp.logical_and(k == 0, i > 0), jnp.logical_and(k == 1, i < 7))
-            for dj, low, size, to in rows:
-                turn = {0: 0, 1: 1, -1: 2}[dj]
-                okj = jnp.logical_and(j - dj >= 0, j - dj < NJ)
-                ok = jnp.logical_and(beside, okj)
-                w = halo if dj == 0 else corner
-                a0 = (5 - w) * (1 - k) + 13 * k
+            a0 = (5 - halo) * (1 - k) + 13 * k
+
+            @pl.when(beside)
+            def _():
                 for half in (0, 1):
-                    pl.when(ok)(copy(0, 1 + 2 * turn + half, 0, w, a0, low, size, to, half, (i, j, other)).wait_recv)
+                    copy(0, 1 + half, 0, halo, a0, 0, 64, 16, half, (i, j, other)).wait_recv()
+
+            for t, dj, to in turns:
+
+                @pl.when(jnp.logical_and(beside, jnp.logical_and(j - dj >= 0, j - dj < NJ)))
+                def _():
+                    for half in (0, 1):
+                        outer_rows(0, 3 + 2 * t + half, yd.at[at, t, 0], rd.at[at, t, half], (i, j, other)).wait_recv()
+                    unpack(rd, t, to, 1 + 12 * k, 4)
 
         def drain():
             for ok, c in inner + sends:
@@ -742,8 +782,9 @@
     scratch += [buf(16, 64, 128)] * 13
     scratch += [buf(16, 96, 128)] * 13 + [buf(16, 40, 128), buf(16, 16, 128)]
     scratch += [buf(18, 56, 128)] * 12 + [buf(18, 8, 128)] * 2
+    scratch += [buf(3, 2, 16, 8, 128)] + [buf(3, 2, 2, 64, 128), buf(3, 2, 2, 24, 128)] * 2
     dma = pltpu.SemaphoreType.DMA
-    scratch += [dma((SEMS,)), dma((3,))]
+    scratch += [dma((SEMS,)), dma((9,))]
     return pl.pallas_call(
         kernel,
         out_shape=pltpu.VMEM((16, 64, 128), F32),

time: 65.7 us -> 63.2 us (0.962)
  Pallas kernels: 64.8 us -> 62.2 us
    pallas_call x1, Pallas kernels: 64.8 us -> 62.2 us  [on_device(): pl.pallas_call(kernel, out_shape=pltpu.VMEM((16, 64, 128), F32), in_specs...]
where the time goes in v6:
time: 63.2 us; the launch traced here: 63 us
  Pallas kernels  62.2 us (98%)
  local copies, waits for them, and re-layouts  0.8 us (1%)
    pallas_call x1, Pallas kernels, on_device(): pl.pallas_call(kernel, out_shape=pltpu.VMEM((16, 64, 128), F32), in_specs...  62.2 us

profile of v6, /device:TPU:5, one launch (start us, length us, event | category | flops | bytes accessed | tf_op | source)
XLA Modules:
  0.0 63.0 jit_solution(14918485929299620577)
XLA Ops:
  0.0 62.2 %vcycle.1 = f32[16,64,128]{2,1,0:T(8,128)S(1)} custom-call(f32[16,64,128]{2,1,0:T(8,128)} %iterate.1, f32[16,64,128]{2,1,0:T(8,128)} %right_side.1, f32[16,64,128]{2,1,0:T(8,128)} %diffusion.1), custom_call_target="tpu_custom_call" | custom-call | flops 100000000 | bytes 2000000 | tf_op jit(solution)/shard_map/vcycle/pallas_call | solution.py:788
  62.2 0.8 %copy.5 = f32[16,64,128]{2,1,0:T(8,128)} copy(f32[16,64,128]{2,1,0:T(8,128)S(1)} %vcycle.1) | data formatting | bytes 1048576

commit v7 on v6

--- a/solution.py
+++ b/solution.py
@@ -183,16 +183,27 @@
     for load in faces:
         load.wait()
 
-    def pack_faces(at):
-        for t, low in enumerate((3, 0)):
-            for m in range(12):
-                for half in range(2):
-                    yb[at, t, half, 5 * m:5 * m + 5] = face[at, t, m + 4 * half, low:low + 5]
-            for m in range(4):
-                for end in range(2):
-                    yd[at, t, end, 5 * m:5 * m + 5] = face[at, t, m + 12 * (1 - end), low:low + 5]
-
-    loop(0, 3, pack_faces)
+    def strips(at, planes):
+        halo = 4 if at == 2 else 5
+        res, start = [], 0
+        for m, steps in enumerate(planes):
+            if halo > steps:
+                res.append((m, start, halo - steps))
+                start += halo - steps
+        return res, -(-start // 8) * 8
+
+    near = ((0,) * 8 + (1, 2, 3, 4), (4, 3, 2, 1) + (0,) * 8)
+    corners = ((4, 3, 2, 1), (1, 2, 3, 4))
+    for at in range(3):
+        for t in range(2):
+            for half in range(2):
+                for m, start, rows in strips(at, near[half])[0]:
+                    low = (1 - t) * (8 - rows)
+                    yb[at, t, half, start:start + rows] = face[at, t, m + 4 * half, low:low + rows]
+                for m, start, rows in strips(at, corners[half])[0]:
+                    low = (1 - t) * (8 - rows)
+                    yd[at, t, half, start:start + rows] = face[at, t, m + 12 * (1 - half), low:low + rows]
+
     pl.semaphore_wait(barrier, count)
 
     def fine_moves(at, src, dst, halo):
@@ -228,17 +239,19 @@
         sends = []
         sends.append((i < 7, copy(1, 1 + k, 16 - halo, halo, 5 - halo, 0, 64, 16, k, (i + 1, j, 0))))
         sends.append((i > 0, copy(2, 1 + k, 0, halo, 13, 0, 64, 16, k, (i - 1, j, 1))))
-        turns = ((0, 1, 11), (1, -1, 80))
-        for t, dj, to in turns:
+        turns = ((0, 1), (1, -1))
+        near_rows = pl.ds(0, strips(at, near[0])[1])
+        corner_rows = pl.ds(0, strips(at, corners[0])[1])
+        for t, dj in turns:
             okj = jnp.logical_and(j + dj >= 0, j + dj < NJ)
             up = jnp.logical_and(i < 7, okj)
             down = jnp.logical_and(i > 0, okj)
             slot = 3 + 2 * t
-            sends.append((up, outer_rows(slot, slot + k, yd.at[at, t, 0], rd.at[at, t, k], (i + 1, j + dj, 0))))
-            sends.append((down, outer_rows(slot + 1, slot + k, yd.at[at, t, 1], rd.at[at, t, k], (i - 1, j + dj, 1))))
+            sends.append((up, outer_rows(slot, slot + k, yd.at[at, t, 0, corner_rows], rd.at[at, t, k, corner_rows], (i + 1, j + dj, 0))))
+            sends.append((down, outer_rows(slot + 1, slot + k, yd.at[at, t, 1, corner_rows], rd.at[at, t, k, corner_rows], (i - 1, j + dj, 1))))
             slot = 7 + 2 * t
             for half in (0, 1):
-                inner.append((okj, outer_rows(slot + half, slot + k, yb.at[at, t, half], ry.at[at, t, k], (i, j + dj, half))))
+                inner.append((okj, outer_rows(slot + half, slot + k, yb.at[at, t, half, near_rows], ry.at[at, t, k, near_rows], (i, j + dj, half))))
 
         def start(part):
             if part == 0:
@@ -249,21 +262,26 @@
                 else:
                     pl.when(ok)(c.start)
 
-        def unpack(buf, t, to, first, planes):
-            for half in (0, 1):
-                for m in range(planes):
-                    dst[first + m, half, to:to + 5] = buf[at, t, half, 5 * m:5 * m + 5]
+        def unpack(buf, t, firsts, tables):
+            for mine_half in range(2):
+
+                @pl.when(k == mine_half)
+                def _():
+                    for m, start, rows in strips(at, tables[mine_half])[0]:
+                        low = 16 - rows if t == 0 else 80
+                        for half in (0, 1):
+                            dst[firsts[mine_half] + m, half, low:low + rows] = buf[at, t, half, start:start + rows]
 
         def arrive_inner():
             mine.wait()
             copy(0, 0, 0, n, 5 - halo * k, 0, 64, 16, other, (i, j, other)).wait_recv()
-            for t, dj, to in turns:
+            for t, dj in turns:
 
                 @pl.when(jnp.logical_and(j - dj >= 0, j - dj < NJ))
                 def _():
                     for half in (0, 1):
-                        outer_rows(0, 7 + 2 * t + half, yb.at[at, t, 0], ry.at[at, t, half], (i, j, other)).wait_recv()
-                    unpack(ry, t, to, 5 - 4 * k, 12)
+                        outer_rows(0, 7 + 2 * t + half, yb.at[at, t, 0, near_rows], ry.at[at, t, half, near_rows], (i, j, other)).wait_recv()
+                    unpack(ry, t, (5, 1), near)
 
         def arrive_outer():
             beside = jnp.logical_or(jnp.logical_and(k == 0, i > 0), jnp.logical_and(k == 1, i < 7))
@@ -274,13 +292,13 @@
                 for half in (0, 1):
                     copy(0, 1 + half, 0, halo, a0, 0, 64, 16, half, (i, j, other)).wait_recv()
 
-            for t, dj, to in turns:
+            for t, dj in turns:
 
                 @pl.when(jnp.logical_and(beside, jnp.logical_and(j - dj >= 0, j - dj < NJ)))
                 def _():
                     for half in (0, 1):
-                        outer_rows(0, 3 + 2 * t + half, yd.at[at, t, 0], rd.at[at, t, half], (i, j, other)).wait_recv()
-                    unpack(rd, t, to, 1 + 12 * k, 4)
+                        outer_rows(0, 3 + 2 * t + half, yd.at[at, t, 0, corner_rows], rd.at[at, t, half, corner_rows], (i, j, other)).wait_recv()
+                    unpack(rd, t, (1, 13), corners)
 
         def drain():
             for ok, c in inner + sends:
@@ -782,7 +800,7 @@
     scratch += [buf(16, 64, 128)] * 13
     scratch += [buf(16, 96, 128)] * 13 + [buf(16, 40, 128), buf(16, 16, 128)]
     scratch += [buf(18, 56, 128)] * 12 + [buf(18, 8, 128)] * 2
-    scratch += [buf(3, 2, 16, 8, 128)] + [buf(3, 2, 2, 64, 128), buf(3, 2, 2, 24, 128)] * 2
+    scratch += [buf(3, 2, 16, 8, 128)] + [buf(3, 2, 2, 56, 128), buf(3, 2, 2, 16, 128)] * 2
     dma = pltpu.SemaphoreType.DMA
     scratch += [dma((SEMS,)), dma((9,))]
     return pl.pallas_call(

time: 63.2 us -> 61.2 us (0.968)
  Pallas kernels: 62.2 us -> 60.2 us
    pallas_call x1, Pallas kernels: 62.2 us -> 60.2 us  [on_device(): pl.pallas_call(kernel, out_shape=pltpu.VMEM((16, 64, 128), F32), in_specs...]
where the time goes in v7:
time: 61.2 us; the launch traced here: 61 us
  Pallas kernels  60.2 us (98%)
  local copies, waits for them, and re-layouts  0.8 us (1%)
    pallas_call x1, Pallas kernels, on_device(): pl.pallas_call(kernel, out_shape=pltpu.VMEM((16, 64, 128), F32), in_specs...  60.2 us

profile of v7, /device:TPU:5, one launch (start us, length us, event | category | flops | bytes accessed | tf_op | source)
XLA Modules:
  0.0 61.0 jit_solution(1046328965988096863)
XLA Ops:
  0.0 60.2 %vcycle.1 = f32[16,64,128]{2,1,0:T(8,128)S(1)} custom-call(f32[16,64,128]{2,1,0:T(8,128)} %iterate.1, f32[16,64,128]{2,1,0:T(8,128)} %right_side.1, f32[16,64,128]{2,1,0:T(8,128)} %diffusion.1), custom_call_target="tpu_custom_call" | custom-call | flops 100000000 | bytes 2000000 | tf_op jit(solution)/shard_map/vcycle/pallas_call | solution.py:806
  60.3 0.8 %copy.5 = f32[16,64,128]{2,1,0:T(8,128)} copy(f32[16,64,128]{2,1,0:T(8,128)S(1)} %vcycle.1) | data formatting | bytes 1048576
